TPU v7x, 512 devices: a whole 4x8x8 slice. The times are simulated.
512 devices in a mesh: sky: 16 (over y_lo, x, core), uv: 32 (over z, y_hi).
Axes of the slice: x: 4, y: 8 (y_hi: 4, y_lo: 2; y = y_hi * 2 + y_lo), z: 8, core: 2. Of those that a mesh axis runs over, the one named last changes fastest.
Arguments:
- sky_model: bfloat16 [64, 256, 256], P('sky'), may hold values from -6 to 6
- beam: float32 [32, 4, 16, 2, 256], P('uv'), may hold values from 0.25 to 1
- tile_anchor: int32 [64, 2], replicated, may hold values from 0 to 63
- coverage: int32 [32, 16], P('uv'), may hold values from 0 to 63, as said below
- unit_chan: int32 [32, 16], P('uv'), may hold values from 0 to 3
- unit_block: int32 [32, 16, 2], P('uv'), may hold values from 0 to 63
- unit_occupied_mask: int32 [32, 16], P('uv'), may hold values 0 or 1
- observed: bfloat16 [32, 16, 2, 256, 256], P('uv', 'sky'), may hold values from -12 to 12
Outputs:
- residual_vis: bfloat16 [32, 16, 2, 256, 256], P('uv', 'sky')
- residual_image: bfloat16 [64, 256, 256], P('sky')
Inputs may be any that keep to these rules, and one draw needn't show every extreme that they name: `coverage`: slot k of every pointing's list names one of the tiles of sky index k: a number from k * 4 to k * 4 + 3.
All inputs are finite; a program needn't handle non-finite values. No bound on the sum of `unit_occupied_mask` on one device may be relied on, other than what follows from the above.
Results may differ from a plain program's by a relative error of at most 0.02.
Values may be sent and summed in bfloat16 or wider, within the bound.
No kernel may reach another device: no remote copies, remote signals or barrier semaphores. Data moves between devices by JAX's collectives and lax.ppermute only.
A program may use at most 64 MiB of HBM per device.

v0:
```python
import math

import jax
import jax.numpy as jnp
from jax import lax
from jax.sharding import PartitionSpec as P

PIXELS = 256
GRID_TILES = 64


def phase_tables(offset, anchor):
    counter = jnp.arange(PIXELS, dtype=jnp.int32)
    frequency = offset + GRID_TILES * counter
    coords = PIXELS * anchor + counter
    product = frequency[:, None] * coords[None, :] % (GRID_TILES * PIXELS)
    angles = product.astype(jnp.float32) * (2.0 * math.pi / (GRID_TILES * PIXELS))
    factor = PIXELS ** (-0.5)
    return (
        (jnp.cos(angles) * factor).astype(jnp.bfloat16),
        (jnp.sin(angles) * factor).astype(jnp.bfloat16),
    )


def apply_beam(sky_tile, profiles):
    shaped = profiles[0][:, None] * profiles[1][None, :]
    return (sky_tile.astype(jnp.float32) * shaped).astype(jnp.bfloat16)


def predict(weighted, tables):
    cos_rows, sin_rows, cos_cols, sin_cols = tables
    stacked_cols = jnp.concatenate([cos_cols, sin_cols], axis=0)
    partial_rows = jnp.dot(weighted, stacked_cols.T, preferred_element_type=jnp.float32).astype(
        jnp.bfloat16
    )
    stacked_rows = jnp.concatenate([cos_rows, sin_rows], axis=0)
    blocks = jnp.dot(stacked_rows, partial_rows, preferred_element_type=jnp.float32)
    real_part = blocks[:PIXELS, :PIXELS] - blocks[PIXELS:, PIXELS:]
    imag_part = -(blocks[PIXELS:, :PIXELS] + blocks[:PIXELS, PIXELS:])
    return jnp.stack([real_part, imag_part])


def regrid(residual_value, tables):
    cos_rows, sin_rows, cos_cols, sin_cols = tables
    left_table = jnp.concatenate(
        [
            jnp.concatenate([cos_rows, sin_rows], axis=1),
            jnp.concatenate([-sin_rows, cos_rows], axis=1),
        ],
        axis=0,
    )
    stacked_planes = jnp.concatenate([residual_value[0], residual_value[1]], axis=0)
    turned = jnp.dot(left_table.T, stacked_planes, preferred_element_type=jnp.float32).astype(
        jnp.bfloat16
    )
    joined = jnp.concatenate([turned[:PIXELS], turned[PIXELS:]], axis=1)
    right_table = jnp.concatenate([cos_cols, -sin_cols], axis=0)
    return jnp.dot(joined, right_table, preferred_element_type=jnp.float32)


def beam_outer(profiles):
    return profiles[0][:, None] * profiles[1][None, :]


def per_device(
    sky_model, beam, tile_anchor, coverage, unit_chan, unit_block, unit_occupied_mask, observed
):
    sky_tile_index = lax.axis_index("sky")
    tiles_here = sky_model.shape[0]
    own_target = coverage[0, sky_tile_index]
    own_position = own_target - sky_tile_index * tiles_here
    own_tile = lax.dynamic_index_in_dim(sky_model, own_position, 0, keepdims=False)
    beam_here = beam[0]
    channel = unit_chan[0, sky_tile_index]
    block_first = unit_block[0, sky_tile_index, 0]
    block_second = unit_block[0, sky_tile_index, 1]
    unit_presence = unit_occupied_mask[0, sky_tile_index]
    channel_beam = lax.dynamic_index_in_dim(beam_here, channel, 0, keepdims=False)
    empty_sky_model = jnp.zeros((2, PIXELS, PIXELS), jnp.float32)

    def slot_tables(slot_index):
        target = coverage[0, slot_index]
        return phase_tables(block_first, tile_anchor[target, 0]) + phase_tables(
            block_second, tile_anchor[target, 1]
        )

    own_profiles = lax.dynamic_index_in_dim(beam_here, sky_tile_index, 1, keepdims=False)
    outgoing = jax.vmap(apply_beam, in_axes=(None, 0))(own_tile, own_profiles)[None]
    received = lax.all_gather(outgoing, "sky", axis=0, tiled=True)

    def add_one(offset, model_total_sum):
        every_channel = lax.dynamic_index_in_dim(received, offset, 0, keepdims=False)
        weighted = lax.dynamic_index_in_dim(every_channel, channel, 0, keepdims=False)
        return model_total_sum + predict(weighted, slot_tables(offset))

    model_total_sum = lax.cond(
        unit_presence > 0,
        lambda: lax.fori_loop(0, received.shape[0], add_one, empty_sky_model),
        lambda: empty_sky_model,
    )
    residual_value = (
        (observed[0, 0].astype(jnp.float32) - model_total_sum) * unit_presence.astype(jnp.float32)
    ).astype(jnp.bfloat16)

    def one_slot(offset):
        profiles = lax.dynamic_index_in_dim(channel_beam, offset, 0, keepdims=False)
        return regrid(residual_value, slot_tables(offset)) * beam_outer(profiles)

    own_image = lax.psum_scatter(
        lax.cond(
            unit_presence > 0,
            lambda: lax.map(one_slot, jnp.arange(1 * lax.axis_size("sky"), dtype=jnp.int32)),
            lambda: jnp.zeros((1 * lax.axis_size("sky"), PIXELS, PIXELS), jnp.float32),
        ).astype(jnp.bfloat16),
        "sky",
        scatter_dimension=0,
        tiled=True,
    ).astype(jnp.float32)[0]
    selector = (jnp.arange(tiles_here, dtype=jnp.int32) == own_position).astype(jnp.float32)
    spread = selector[:, None, None] * own_image[None]
    summed = lax.psum(spread.astype(jnp.bfloat16), "uv")
    return (residual_value[None, None], summed)


def solution(mesh):
    placed = (
        P("sky", None, None),
        P("uv", None, None, None, None),
        P(),
        P("uv", None),
        P("uv", None),
        P("uv", None, None),
        P("uv", None),
        P("uv", "sky", None, None, None),
    )
    return jax.shard_map(
        per_device,
        mesh=mesh,
        in_specs=placed,
        out_specs=(P("uv", "sky", None, None, None), P("sky", None, None)),
        check_vma=False,
    )
```

profile of v0, /device:TPU:2, one launch (start us, length us, event | category | flops | bytes accessed | tf_op | source)
XLA Modules:
  0.0 937.5 jit_solution(7666967396973574872)
XLA Ops:
  16.5 57.5 %all-gather.2.cloned.1.call-done = bf16[16,4,256,256]{3,2,1,0:T(8,128)(2,1)} async-done(((bf16[1,4,256,256]{3,2,1,0:T(8,128)(2,1)}), bf16[16,4,256,256]{3,2,1,0:T(8,128)(2,1)}) %all-gather.2.cloned.1.call-update) | async-done | bytes 8388624 | tf_op jit(solution)/shard_map/all_gather | solution.py:89
  74.0 211.7 %conditional.2 = (f32[2,256,256]{2,1,0:T(8,128)}) conditional(s32[]{:T(128)} %bitcast.11, () %tuple.60, (s32[]{:T(128)}, s32[]{:T(128)}, s32[1,16]{1,0:T(1,128)}, s32[64,2]{0,1:T(2,128)}, bf16[16,4,256,256]{3,2,1,0:T(8,128)(2,1)}, /*index=5*/s32[]{:T(128)}) %tuple.61), branch_computations={%region_0.1_spmd, %region_1.4_spmd} | conditional | flops 205456640 | bytes 5383087 | solution.py:96
  76.2 209.5 %while.29 = (s32[]{:T(128)}, f32[2,256,256]{2,1,0:T(8,128)}, s32[]{:T(128)}, s32[1,16]{1,0:T(1,128)}, s32[64,2]{0,1:T(2,128)}, /*index=5*/bf16[16,4,256,256]{3,2...) while((s32[]{:T(128)}, f32[2,256,256]{2,1,0:T(8,128)}, ...), condition=%wide.region_3.3_spmd.clone, body=%wide.region_2.2_spmd.clone.sunk | while | flops 205456640 | bytes 5382917 | solution.py:98
  99.5 1.9 maximum_add_fusion.2
  112.7 1.9 maximum_add_fusion.2
  125.8 1.9 maximum_add_fusion.2
  139.0 1.9 maximum_add_fusion.2
  150.6 1.4 fusion.90
  152.1 1.9 maximum_add_fusion.2
  163.8 1.4 fusion.90
  165.3 1.9 maximum_add_fusion.2
  176.9 1.4 fusion.90
  178.5 1.9 maximum_add_fusion.2
  191.6 1.9 maximum_add_fusion.2
  203.3 1.4 fusion.90
  204.8 1.9 maximum_add_fusion.2
  216.4 1.4 fusion.90
  217.9 1.9 maximum_add_fusion.2
  229.6 1.4 fusion.90
  231.1 1.9 maximum_add_fusion.2
  242.7 1.4 fusion.90
  244.3 1.9 maximum_add_fusion.2
  255.9 1.4 fusion.90
  257.4 1.9 maximum_add_fusion.2
  270.6 1.9 maximum_add_fusion.2
  283.8 1.9 maximum_add_fusion.2
  285.7 1.8 fusion.57
  287.5 252.1 %conditional.3 = (bf16[16,256,256]{2,1,0:T(8,128)(2,1)}) conditional(s32[]{:T(128)} %bitcast.11, () %tuple.62, (s32[]{:T(128)}, f32[1,4,16,2,256]{4,3,2,1,0:T(2,128)}, bf16[2,256,256]{2,1,0:T(8,128)(2,1)}, s32[]{:T(128)}, s32[1,16]{1,0:T(1,128)}, /*index=5*/s32[64,2]{0,1:T(2,128)}, s32[]{:T(128)}) %tuple.63), branch_computations={%region_4.5_spmd, %region_5.8_spmd} | conditional | flops 209978624 | bytes 4017191 | solution.py:110
  291.4 248.2 %while.30 = (s32[]{:T(128)}, bf16[16,256,256]{2,1,0:T(8,128)(2,1)}, s32[]{:T(128)}, s32[16]{0:T(128)S(1)}, s32[1,16]{1,0:T(1,128)}, /*index=5*/s32[64,2]{0,1:T(2...) while((s32[]{:T(128)}, bf16[16,256,256]{2,1,0:T(8,128)(2,1)}, ...), condition=%wide.region_7.7_spmd, body=%wide.region_6.6_spmd.sunk | while | flops 209454336 | bytes 2902841 | solution.py:112
  539.7 65.7 %reduce-scatter.2.cloned.1.call-done = bf16[1,256,256]{2,1,0:T(8,128)(2,1)} async-done(((bf16[16,256,256]{2,1,0:T(8,128)(2,1)}), bf16[1,256,256]{2,1,0:T(8,128)(2,1)}) %reduce-scatter.2.cloned.1.call-update) | async-done | bytes 131088 | tf_op jit(solution)/shard_map/reduce_scatter | solution.py:109
  607.3 321.8 %all-reduce.2.cloned.1.call-done = bf16[4,256,256]{2,1,0:T(8,128)(2,1)} async-done(((bf16[4,256,256]{2,1,0:T(8,128)(2,1)}), bf16[4,256,256]{2,1,0:T(8,128)(2,1)}) %all-reduce.2.cloned.1.call-update) | async-done | bytes 524304 | tf_op jit(solution)/shard_map/psum | solution.py:121
  929.1 1.9 copy.32
  (389 shorter events, 295.5 us)
Async XLA Ops:
  7.2 4.7 copy-start
  7.2 66.8 %all-gather.2.cloned.1.call-start = ((), (), s32[]{:S(2)}) async-start(), calls=%async_computation.1 | async-start | bytes 8912896 | tf_op jit(solution)/shard_map/all_gather | solution.py:89
  11.8 593.6 %reduce-scatter.2.cloned.1.call-start = ((), (), s32[]{:S(2)}) async-start(), calls=%async_computation.2 | async-start | bytes 2228224 | tf_op jit(solution)/shard_map/reduce_scatter | solution.py:109
  74.0 211.7 %copy-start.1 = (bf16[1,1,2,256,256]{4,3,2,1,0:T(8,128)(2,1)S(1)}, bf16[1,1,2,256,256]{4,3,2,1,0:T(8,128)(2,1)}, u32[]{:S(2)}) copy-start(bf16[1,1,2,256,256]{4,3,2,1,0:T(8,128)(2,1)} %param.23) | copy-start | bytes 786436
  539.6 389.5 %all-reduce.2.cloned.1.call-start = ((), (), s32[]{:S(2)}) async-start(), calls=%async_computation.3 | async-start | bytes 1048576 | tf_op jit(solution)/shard_map/psum | solution.py:121
Sparse Core Ops, SparseCore 0:
  11.9 62.0 all-gather.1
  539.8 65.5 reduce-scatter.1
  608.9 320.1 all-reduce.1
where the time goes:
time: 942 us; the launch traced here: 937 us
  waiting for transfers between devices  445 us (47%)
  other arithmetic  193 us (20%)
  loops' own time  137 us (15%)
  local copies, waits for them, and re-layouts  103 us (11%)
  matrix products  43.4 us (5%)
  between operations  15.7 us (2%)
    psum x1, waiting for transfers between devices, per_device(): summed = lax.psum(spread.astype(jnp.bfloat16), 'uv')  322 us
    another operation x1, loops' own time, per_device(): lax.map(one_slot, jnp.arange(1 * lax.axis_size('sky'), dtype=jnp.int32))  82.3 us
    reduce_scatter x1, waiting for transfers between devices, per_device(): lax.psum_scatter(lax.cond(unit_presence > 0, lambda: lax.map(one_slot, jn...  65.7 us
    convert_element_type x48, other arithmetic, phase_tables(): (jnp.cos(angles) * factor).astype(jnp.bfloat16)  57.7 us
    all_gather x1, waiting for transfers between devices, per_device(): received = lax.all_gather(outgoing, 'sky', axis=0, tiled=True)  57.5 us
    another operation x1, loops' own time, per_device(): lax.fori_loop(0, received.shape[0], add_one, empty_sky_model)  50.4 us
    dynamic_slice x32, local copies, waits for them, and re-layouts, slot_tables(): tile_anchor[target, 1]  44.3 us
    add x32, other arithmetic, phase_tables(): frequency = offset + GRID_TILES * counter  42.5 us
  transfers between devices with their start and end apart: 3, of which 3 were waited for; matrix products, arithmetic and copies ran while one was open for 0% of the time, Pallas kernels for 0%

commit v1 on v0

v1 whole, which is shorter than its diff:
```python
import math

import jax
import jax.numpy as jnp
import numpy as np
from jax import lax
from jax.experimental import pallas as pl
from jax.experimental.pallas import tpu as pltpu
from jax.sharding import Mesh, PartitionSpec as P

PIXELS = 256
GRID_TILES = 64
TURN = GRID_TILES * PIXELS
TILES_DEV = 4
CHIPS = 8
CORES = 2
UNITS = CHIPS * CORES
ROWS = 16
BF = jnp.bfloat16
F32 = jnp.float32

SMEM = pl.BlockSpec(memory_space=pltpu.SMEM)
VMEM = pl.BlockSpec(memory_space=pltpu.VMEM)


def dft_matrix():
    counter = np.arange(PIXELS)
    angles = 2.0 * np.pi * (counter[:, None] * counter[None, :] % PIXELS) / PIXELS
    return jnp.asarray(np.stack([np.cos(angles), np.sin(angles)]) / math.sqrt(PIXELS), BF)


def anchor_roots():
    angles = 2.0 * np.pi * np.arange(GRID_TILES) / GRID_TILES
    return jnp.asarray(np.stack([np.cos(angles), np.sin(angles)]), F32)


def dot(left, right):
    return jnp.dot(left, right, preferred_element_type=F32)


def slot_phase(coverage, anchors, blocks, roots, unit, slot):
    tile = coverage[0, slot]
    turns = blocks[0, unit, 0] * anchors[tile, 0] + blocks[0, unit, 1] * anchors[tile, 1]
    turns = lax.bitwise_and(turns, GRID_TILES - 1)
    return roots[0, turns], roots[1, turns]


def load_profiles(chans, beam, units, core, firsts, seconds):
    lines = []
    for unit in units:
        channel = chans[0, unit]
        for chip in range(CHIPS):
            pair = beam[0, channel, 2 * chip + core]
            lines.append(pair[0:1])
            seconds[len(lines) - 1 : len(lines), :] = pair[1:2]
    firsts[...] = jnp.transpose(jnp.concatenate(lines, axis=0))


def combine_kernel(
    place, coverage, chans, blocks, anchors, roots, tiles, beam, own, other, firsts, seconds
):
    sky = place[0]
    core = lax.bitwise_and(sky, 1)
    units = (sky, lax.bitwise_xor(sky, 1))
    load_profiles(chans, beam, units, core, firsts, seconds)
    phases = [
        [slot_phase(coverage, anchors, blocks, roots, unit, 2 * chip + core) for chip in range(CHIPS)]
        for unit in units
    ]

    @pl.loop(0, PIXELS // ROWS)
    def step(at):
        rows = pl.ds(pl.multiple_of(at * ROWS, ROWS), ROWS)
        first = firsts[rows, :]
        sums = [[jnp.zeros((ROWS, PIXELS), F32) for _ in range(2)] for _ in units]
        for chip in range(CHIPS):
            tile = tiles[chip, rows, :].astype(F32)
            for e in range(2):
                line = e * CHIPS + chip
                weighted = tile * seconds[line : line + 1, :] * first[:, line : line + 1]
                cosine, sine = phases[e][chip]
                sums[e][0] += cosine * weighted
                sums[e][1] += sine * weighted
        for plane in range(2):
            own[plane, rows, :] = sums[0][plane]
            other[plane, rows, :] = sums[1][plane].astype(BF)


def twiddles(offset):
    turns = lax.bitwise_and(offset * lax.broadcasted_iota(jnp.int32, (8, PIXELS), 1), TURN - 1)
    angles = turns.astype(F32) * (2.0 * math.pi / TURN)
    return jnp.cos(angles), jnp.sin(angles)


def unit_kernel(place, blocks, masks, own, arrived, observed, table, residual, turned, shift):
    sky = place[0]
    col_cos, col_sin = twiddles(blocks[0, sky, 1])
    row_cos, row_sin = twiddles(blocks[0, sky, 0])
    row_cos, row_sin = jnp.transpose(row_cos)[:, 0:1], jnp.transpose(row_sin)[:, 0:1]
    col_cos, col_sin = col_cos[0:1], col_sin[0:1]
    shift[0] = row_cos * col_cos - row_sin * col_sin
    shift[1] = row_sin * col_cos + row_cos * col_sin

    sum_re = own[0] + arrived[0].astype(F32)
    sum_im = own[1] + arrived[1].astype(F32)
    sky_re = (sum_re * shift[0] - sum_im * shift[1]).astype(BF)
    sky_im = (sum_re * shift[1] + sum_im * shift[0]).astype(BF)
    cosines, sines = table[0], table[1]
    part_re = (dot(sky_re, cosines) - dot(sky_im, sines)).astype(BF)
    part_im = (dot(sky_re, sines) + dot(sky_im, cosines)).astype(BF)
    model_re = dot(cosines, part_re) - dot(sines, part_im)
    model_im = -(dot(sines, part_re) + dot(cosines, part_im))

    occupied = masks[0, sky].astype(F32)
    res_re = (occupied * (observed[0, 0, 0].astype(F32) - model_re)).astype(BF)
    res_im = (occupied * (observed[0, 0, 1].astype(F32) - model_im)).astype(BF)
    residual[0, 0, 0] = res_re
    residual[0, 0, 1] = res_im
    part_re = (dot(cosines, res_re) - dot(sines, res_im)).astype(BF)
    part_im = (dot(sines, res_re) + dot(cosines, res_im)).astype(BF)
    back_re = dot(part_re, cosines) - dot(part_im, sines)
    back_im = dot(part_re, sines) + dot(part_im, cosines)
    turned[0, 0] = (back_re * shift[0] - back_im * shift[1]).astype(BF)
    turned[0, 1] = (back_re * shift[1] + back_im * shift[0]).astype(BF)


def spread_kernel(
    place, coverage, chans, blocks, anchors, roots, turned, beam, images, firsts, seconds
):
    sky = place[0]
    core = lax.bitwise_and(sky, 1)
    units = (sky - core, sky - core + 1)
    load_profiles(chans, beam, units, core, firsts, seconds)
    phases = [
        [slot_phase(coverage, anchors, blocks, roots, unit, 2 * chip + core) for chip in range(CHIPS)]
        for unit in units
    ]

    @pl.loop(0, PIXELS // ROWS)
    def step(at):
        rows = pl.ds(pl.multiple_of(at * ROWS, ROWS), ROWS)
        first = firsts[rows, :]
        planes = [[turned[e, plane, rows, :].astype(F32) for plane in range(2)] for e in range(2)]
        for chip in range(CHIPS):
            total = None
            for e in range(2):
                line = e * CHIPS + chip
                cosine, sine = phases[e][chip]
                part = cosine * planes[e][0] - sine * planes[e][1]
                part = part * seconds[line : line + 1, :] * first[:, line : line + 1]
                total = part if total is None else total + part
            images[chip, rows, :] = total.astype(BF)


def gather_kernel(place, coverage, parts, spread):
    sky = place[0]
    position = coverage[0, sky] - sky * TILES_DEV
    for other in range(TILES_DEV):
        spread[other] = jnp.zeros((PIXELS, PIXELS), BF)

    @pl.loop(0, PIXELS // ROWS)
    def step(at):
        rows = pl.ds(pl.multiple_of(at * ROWS, ROWS), ROWS)
        total = parts[0, rows, :].astype(F32)
        for chip in range(1, CHIPS):
            total += parts[chip, rows, :].astype(F32)
        spread[position, rows, :] = total.astype(BF)


def total_kernel(parts, repeated):
    pointings = parts.shape[0]
    total = parts[0].astype(F32)
    for p in range(1, pointings):
        total += parts[p].astype(F32)
    total = total.astype(BF)
    for p in range(pointings):
        repeated[p] = total


def shape(dims, kind):
    return jax.ShapeDtypeStruct(dims, kind)


def per_device(
    sky_model, beam, tile_anchor, coverage, unit_chan, unit_block, unit_occupied_mask, observed
):
    chip_core = lax.axis_index("chip") * CORES + lax.axis_index("core")
    place = chip_core.astype(jnp.int32).reshape(1)
    pointings = lax.axis_size("uv")
    roots = anchor_roots()
    profiles = [pltpu.VMEM((PIXELS, UNITS), F32), pltpu.VMEM((UNITS, PIXELS), F32)]

    own_position = coverage[0, chip_core] - chip_core * TILES_DEV
    own_tile = lax.dynamic_index_in_dim(sky_model, own_position, 0, keepdims=True)
    copies = jnp.broadcast_to(own_tile, (CHIPS, PIXELS, PIXELS))
    tiles = lax.all_to_all(copies, "chip", 0, 0, tiled=True)

    own, other = pl.pallas_call(
        combine_kernel,
        out_shape=(shape((2, PIXELS, PIXELS), F32), shape((2, PIXELS, PIXELS), BF)),
        in_specs=[SMEM] * 6 + [VMEM] * 2,
        out_specs=(VMEM, VMEM),
        scratch_shapes=profiles,
        name="combine",
    )(place, coverage, unit_chan, unit_block, tile_anchor, roots, tiles, beam)
    arrived = lax.ppermute(other, "core", [(0, 1), (1, 0)])

    residual, turned = pl.pallas_call(
        unit_kernel,
        out_shape=(
            shape((1, 1, 2, PIXELS, PIXELS), BF),
            shape((1, 2, PIXELS, PIXELS), BF),
        ),
        in_specs=[SMEM] * 3 + [VMEM] * 4,
        out_specs=(VMEM, VMEM),
        scratch_shapes=[pltpu.VMEM((2, PIXELS, PIXELS), F32)],
        name="unit",
    )(place, unit_block, unit_occupied_mask, own, arrived, observed, dft_matrix())
    both = lax.all_gather(turned, "core", axis=0, tiled=True)

    images = pl.pallas_call(
        spread_kernel,
        out_shape=shape((CHIPS, PIXELS, PIXELS), BF),
        in_specs=[SMEM] * 6 + [VMEM] * 2,
        out_specs=VMEM,
        scratch_shapes=profiles,
        name="spread",
    )(place, coverage, unit_chan, unit_block, tile_anchor, roots, both, beam)
    parts = lax.all_to_all(images, "chip", 0, 0, tiled=True)

    spread = pl.pallas_call(
        gather_kernel,
        out_shape=shape((TILES_DEV, PIXELS, PIXELS), BF),
        in_specs=[SMEM] * 2 + [VMEM],
        out_specs=VMEM,
        name="gather",
    )(place, coverage, parts)
    share = TILES_DEV * PIXELS // pointings
    spread = spread.reshape(pointings, share, PIXELS)
    shares = lax.all_to_all(spread, "uv", 0, 0, tiled=True)

    repeated = pl.pallas_call(
        total_kernel,
        out_shape=shape((pointings, share, PIXELS), BF),
        in_specs=[VMEM],
        out_specs=VMEM,
        name="total",
    )(shares)
    image = lax.all_to_all(repeated, "uv", 0, 0, tiled=True)
    return residual, image.reshape(TILES_DEV, PIXELS, PIXELS)


def solution(mesh):
    pointings = mesh.shape["uv"]
    fine = Mesh(mesh.devices.reshape(CHIPS, CORES, pointings), ("chip", "core", "uv"))
    sky = ("chip", "core")
    return jax.shard_map(
        per_device,
        mesh=fine,
        in_specs=(
            P(sky, None, None),
            P("uv", None, None, None, None),
            P(),
            P("uv", None),
            P("uv", None),
            P("uv", None, None),
            P("uv", None),
            P("uv", sky, None, None, None),
        ),
        out_specs=(P("uv", sky, None, None, None), P(sky, None, None)),
        check_vma=False,
    )
```

time: 942 us -> 131 us (0.14)
  the two profiles are of different devices: /device:TPU:2 before, /device:TPU:14 now
where the time goes in v1:
time: 131 us; the launch traced here: 130 us
  blocking collectives  85.4 us (65%)
  Pallas kernels  16.5 us (13%)
  starting transfers between devices  11.3 us (9%)
  waiting for transfers between devices  9.78 us (7%)
  local copies, waits for them, and re-layouts  6.22 us (5%)
  between operations  1.34 us (1%)
    all_to_all x1, blocking collectives, per_device(): shares = lax.all_to_all(spread, 'uv', 0, 0, tiled=True)  36 us
    all_to_all x1, blocking collectives, per_device(): image = lax.all_to_all(repeated, 'uv', 0, 0, tiled=True)  24.4 us
    all_to_all x1, blocking collectives, per_device(): parts = lax.all_to_all(images, 'chip', 0, 0, tiled=True)  19.8 us
    all_to_all x1, starting transfers between devices, per_device(): tiles = lax.all_to_all(copies, 'chip', 0, 0, tiled=True)  9.37 us
    all_to_all x1, waiting for transfers between devices, per_device(): tiles = lax.all_to_all(copies, 'chip', 0, 0, tiled=True)  8.07 us
    all_gather x1, blocking collectives, per_device(): both = lax.all_gather(turned, 'core', axis=0, tiled=True)  5.1 us
    unnamed x15, local copies, waits for them, and re-layouts  4.58 us
    pallas_call x1, Pallas kernels, per_device(): pl.pallas_call(spread_kernel, out_shape=shape((CHIPS, PIXELS, PIXELS), BF...  4.5 us
  transfers between devices with their start and end apart: 2, of which 2 were waited for; matrix products, arithmetic and copies ran while one was open for 1% of the time, Pallas kernels for 0%

profile of v1, /device:TPU:14, one launch (start us, length us, event | category | flops | bytes accessed | tf_op | source)
XLA Modules:
  0.0 130.5 jit_solution(9537156365821877808)
XLA Ops:
  0.6 0.0 copy-start
  0.7 0.0 copy-start.3
  0.7 0.7 copy-done.3
  1.4 0.6 constant_dynamic-slice_fusion
  2.6 0.0 copy-done
  2.6 1.0 broadcast_in_dim.8
  3.7 0.0 copy-start.4
  3.7 9.4 %all-to-all-start = ((bf16[8,256,256]{2,1,0:T(8,128)(2,1)}), bf16[8,256,256]{2,1,0:T(8,128)(2,1)S(1)}, u32[]{:S(2)}, u32[]{:S(2)}) async-start(bf16[8,256,256]{2,1,0:T(8,128)(2,1)} %broadcast_in_dim.8), calls=%async_computation | async-start | bytes 2097152 | tf_op jit(solution)/shard_map/all_to_all | solution.py:196
  13.1 0.0 copy-done.4
  13.1 0.0 copy-start.5
  13.1 0.7 copy.19.blocks
  13.7 0.0 copy-done.5
  13.7 0.7 copy.18.anchors
  14.4 8.1 %all-to-all-done.tiles = bf16[8,256,256]{2,1,0:T(8,128)(2,1)S(1)} async-done(((bf16[8,256,256]{2,1,0:T(8,128)(2,1)}), bf16[8,256,256]{2,1,0:T(8,128)(2,1)S(1)}, u32[]{:S(2)}, u32[]{:S(2)}) %all-to-all-start) | async-done | bytes 1048608 | tf_op jit(solution)/shard_map/all_to_all | solution.py:196
  22.5 0.0 copy-start.1
  22.5 1.0 copy-done.1
  23.5 4.4 %combine.1 = (f32[2,256,256]{2,1,0:T(8,128)}, bf16[2,256,256]{2,1,0:T(8,128)(2,1)}) custom-call(s32[1]{0:T(128)} %bitcast.place, s32[1,16]{1,0:T(1,128)} %coverage.5, s32[1,16]{1,0:T(1,128)} %chans.3, s32[1,16,2]{2,1,0:T(8,128)} %copy.19.blocks, s32[64,2]{1,0:T(8,128)} %copy.18.anchors, f32[2,64]{1,0:T(2,128)} %constant.28.clone.roots, ...), custom_call_target="tpu_custom_call" | custom-call | tf_op jit(solution)/shard_map/combine/pallas_call | solution.py:198
  27.9 1.9 %collective-permute-start = (bf16[2,256,256]{2,1,0:T(8,128)(2,1)}, bf16[2,256,256]{2,1,0:T(8,128)(2,1)S(1)}, u32[]{:S(2)}, u32[]{:S(2)}) collective-permute-start(bf16[2,256,256]{2,1,0:T(8,128)(2,1)} %get-tuple-element.7), channel_id=1, source_target_pairs={{0,32},{32,0},{1,33},{33,1},{2,34},{34,2},{3,35},{35,3},{4,36},{36... | collective-permute-start | bytes 786440 | tf_op jit(solution)/shard_map/ppermute | solution.py:206
  29.8 1.7 %collective-permute-done.arrived = bf16[2,256,256]{2,1,0:T(8,128)(2,1)S(1)} collective-permute-done((bf16[2,256,256]{2,1,0:T(8,128)(2,1)}, bf16[2,256,256]{2,1,0:T(8,128)(2,1)S(1)}, u32[]{:S(2)}, u32[]{:S(2)}) %collective-permute-start) | collective-permute-done | bytes 262176 | tf_op jit(solution)/shard_map/ppermute | solution.py:206
  31.5 0.0 copy-start.2
  31.5 0.7 copy-done.2
  32.2 3.4 %unit.1 = (bf16[1,1,2,256,256]{4,3,2,1,0:T(8,128)(2,1)}, bf16[1,2,256,256]{3,2,1,0:T(8,128)(2,1)}) custom-call(s32[1]{0:T(128)} %bitcast.place, s32[1,16,2]{2,1,0:T(8,128)} %copy.19.blocks, s32[1,16]{1,0:T(1,128)} %masks.1, f32[2,256,256]{2,1,0:T(8,128)} %get-tuple-element.6.own, bf16[2,256,256]{2,1,0:T(8,128)(2,1)} %copy-done.2, ...), custom_call_target="tpu_custom_call" | custom-call | tf_op jit(solution)/shard_map/unit/pallas_call | solution.py:208
  35.6 5.1 %all_gather.3.turned = bf16[2,2,256,256]{3,2,1,0:T(8,128)(2,1)} all-gather(bf16[1,2,256,256]{3,2,1,0:T(8,128)(2,1)} %get-tuple-element.9), channel_id=1, replica_groups=mesh['chip'=8,'core'=2,'uv'=32] {'core'}, dimensions={0}, use_global_device_ids=true | all-gather | bytes 786432 | tf_op jit(solution)/shard_map/all_gather | solution.py:219
  40.7 4.5 %spread.1 = bf16[8,256,256]{2,1,0:T(8,128)(2,1)} custom-call(s32[1]{0:T(128)} %bitcast.place, s32[1,16]{1,0:T(1,128)} %coverage.5, s32[1,16]{1,0:T(1,128)} %chans.3, s32[1,16,2]{2,1,0:T(8,128)} %copy.19.blocks, s32[64,2]{1,0:T(8,128)} %copy.18.anchors, f32[2,64]{1,0:T(2,128)} %constant.28.clone.roots, bf16[2,2,256,256]{3,2,1,0:T(8,128)(2,1)} %all_gather.3.turned, ...), custom_call_target="tpu_custom_call" | custom-call | tf_op jit(solution)/shard_map/spread/pallas_call | solution.py:221
  45.2 19.8 %all_to_all.20.parts = bf16[8,256,256]{2,1,0:T(8,128)(2,1)} all-to-all(bf16[8,256,256]{2,1,0:T(8,128)(2,1)} %spread.1), channel_id=1, replica_groups=mesh['chip'=8,'core'=2,'uv'=32] {'chip'}, dimensions={0} | all-to-all | bytes 2097152 | tf_op jit(solution)/shard_map/all_to_all | solution.py:229
  65.0 2.3 %gather.1 = bf16[4,256,256]{2,1,0:T(8,128)(2,1)} custom-call(s32[1]{0:T(128)} %bitcast.place, s32[1,16]{1,0:T(1,128)} %coverage.5, bf16[8,256,256]{2,1,0:T(8,128)(2,1)} %all_to_all.20.parts), custom_call_target="tpu_custom_call" | custom-call | tf_op jit(solution)/shard_map/gather/pallas_call | solution.py:231
  67.3 36.0 %all_to_all.21.parts = bf16[32,32,256]{2,1,0:T(8,128)(2,1)} all-to-all(bf16[32,32,256]{2,1,0:T(8,128)(2,1)} %bitcast.7), channel_id=1, replica_groups=mesh['chip'=8,'core'=2,'uv'=32] {'uv'}, dimensions={0} | all-to-all | bytes 1048576 | tf_op jit(solution)/shard_map/all_to_all | solution.py:240
  103.3 1.9 %total.1 = bf16[32,32,256]{2,1,0:T(8,128)(2,1)} custom-call(bf16[32,32,256]{2,1,0:T(8,128)(2,1)} %all_to_all.21.parts), custom_call_target="tpu_custom_call" | custom-call | tf_op jit(solution)/shard_map/total/pallas_call | solution.py:242
  105.3 24.4 %all_to_all.22 = bf16[32,32,256]{2,1,0:T(8,128)(2,1)S(1)} all-to-all(bf16[32,32,256]{2,1,0:T(8,128)(2,1)} %total.1), channel_id=1, replica_groups=mesh['chip'=8,'core'=2,'uv'=32] {'uv'}, dimensions={0} | all-to-all | bytes 1048576 | tf_op jit(solution)/shard_map/all_to_all | solution.py:249
  129.7 0.8 copy.23
  (1 shorter events, 0.0 us)
Async XLA Ops:
  0.6 2.0 %copy-start = (bf16[4,256,256]{2,1,0:T(8,128)(2,1)S(1)}, bf16[4,256,256]{2,1,0:T(8,128)(2,1)}, u32[]{:S(2)}) copy-start(bf16[4,256,256]{2,1,0:T(8,128)(2,1)} %param.10) | copy-start | bytes 1572868
  0.7 0.7 copy-start.3
  3.7 9.4 %copy-start.4 = (s32[1,16,2]{1,2,0:T(2,128)S(1)}, s32[1,16,2]{1,2,0:T(2,128)}, u32[]{:S(2)}) copy-start(s32[1,16,2]{1,2,0:T(2,128)} %param.15) | copy-start | bytes 388
  3.7 18.8 %all-to-all-start = ((bf16[8,256,256]{2,1,0:T(8,128)(2,1)}), bf16[8,256,256]{2,1,0:T(8,128)(2,1)S(1)}, u32[]{:S(2)}, u32[]{:S(2)}) async-start(bf16[8,256,256]{2,1,0:T(8,128)(2,1)} %broadcast_in_dim.8), calls=%async_computation | async-start | bytes 2097152 | tf_op jit(solution)/shard_map/all_to_all | solution.py:196
  13.1 0.7 copy-start.5
  22.5 1.0 copy-start.1
  27.9 3.6 %collective-permute-start = (bf16[2,256,256]{2,1,0:T(8,128)(2,1)}, bf16[2,256,256]{2,1,0:T(8,128)(2,1)S(1)}, u32[]{:S(2)}, u32[]{:S(2)}) collective-permute-start(bf16[2,256,256]{2,1,0:T(8,128)(2,1)} %get-tuple-element.7), channel_id=1, source_target_pairs={{0,32},{32,0},{1,33},{33,1},{2,34},{34,2},{3,35},{35,3},{4,36},{36... | collective-permute-start | bytes 786440 | tf_op jit(solution)/shard_map/ppermute | solution.py:206
  31.5 0.7 copy-start.2

commit v2 on v1

--- a/solution.py
+++ b/solution.py
@@ -19,6 +19,8 @@
 BF = jnp.bfloat16
 F32 = jnp.float32
 
+LIMIT = pltpu.CompilerParams(vmem_limit_bytes=12 * 1024 * 1024)
+
 SMEM = pl.BlockSpec(memory_space=pltpu.SMEM)
 VMEM = pl.BlockSpec(memory_space=pltpu.VMEM)
 
@@ -40,7 +42,7 @@
 
 def slot_phase(coverage, anchors, blocks, roots, unit, slot):
     tile = coverage[0, slot]
-    turns = blocks[0, unit, 0] * anchors[tile, 0] + blocks[0, unit, 1] * anchors[tile, 1]
+    turns = blocks[0, 0, unit] * anchors[0, tile] + blocks[0, 1, unit] * anchors[1, tile]
     turns = lax.bitwise_and(turns, GRID_TILES - 1)
     return roots[0, turns], roots[1, turns]
 
@@ -54,6 +56,13 @@
             lines.append(pair[0:1])
             seconds[len(lines) - 1 : len(lines), :] = pair[1:2]
     firsts[...] = jnp.transpose(jnp.concatenate(lines, axis=0))
+
+
+def copies_kernel(place, coverage, tiles, copies):
+    sky = place[0]
+    own = tiles[coverage[0, sky] - sky * TILES_DEV]
+    for chip in range(CHIPS):
+        copies[chip] = own
 
 
 def combine_kernel(
@@ -94,8 +103,8 @@
 
 def unit_kernel(place, blocks, masks, own, arrived, observed, table, residual, turned, shift):
     sky = place[0]
-    col_cos, col_sin = twiddles(blocks[0, sky, 1])
-    row_cos, row_sin = twiddles(blocks[0, sky, 0])
+    col_cos, col_sin = twiddles(blocks[0, 1, sky])
+    row_cos, row_sin = twiddles(blocks[0, 0, sky])
     row_cos, row_sin = jnp.transpose(row_cos)[:, 0:1], jnp.transpose(row_sin)[:, 0:1]
     col_cos, col_sin = col_cos[0:1], col_sin[0:1]
     shift[0] = row_cos * col_cos - row_sin * col_sin
@@ -190,9 +199,17 @@
     roots = anchor_roots()
     profiles = [pltpu.VMEM((PIXELS, UNITS), F32), pltpu.VMEM((UNITS, PIXELS), F32)]
 
-    own_position = coverage[0, chip_core] - chip_core * TILES_DEV
-    own_tile = lax.dynamic_index_in_dim(sky_model, own_position, 0, keepdims=True)
-    copies = jnp.broadcast_to(own_tile, (CHIPS, PIXELS, PIXELS))
+    anchors = tile_anchor.T
+    blocks = jnp.swapaxes(unit_block, 1, 2)
+
+    copies = pl.pallas_call(
+        copies_kernel,
+        out_shape=shape((CHIPS, PIXELS, PIXELS), BF),
+        in_specs=[SMEM] * 2 + [VMEM],
+        out_specs=VMEM,
+        compiler_params=LIMIT,
+        name="copies",
+    )(place, coverage, sky_model)
     tiles = lax.all_to_all(copies, "chip", 0, 0, tiled=True)
 
     own, other = pl.pallas_call(
@@ -201,8 +218,9 @@
         in_specs=[SMEM] * 6 + [VMEM] * 2,
         out_specs=(VMEM, VMEM),
         scratch_shapes=profiles,
+        compiler_params=LIMIT,
         name="combine",
-    )(place, coverage, unit_chan, unit_block, tile_anchor, roots, tiles, beam)
+    )(place, coverage, unit_chan, blocks, anchors, roots, tiles, beam)
     arrived = lax.ppermute(other, "core", [(0, 1), (1, 0)])
 
     residual, turned = pl.pallas_call(
@@ -214,8 +232,9 @@
         in_specs=[SMEM] * 3 + [VMEM] * 4,
         out_specs=(VMEM, VMEM),
         scratch_shapes=[pltpu.VMEM((2, PIXELS, PIXELS), F32)],
+        compiler_params=LIMIT,
         name="unit",
-    )(place, unit_block, unit_occupied_mask, own, arrived, observed, dft_matrix())
+    )(place, blocks, unit_occupied_mask, own, arrived, observed, dft_matrix())
     both = lax.all_gather(turned, "core", axis=0, tiled=True)
 
     images = pl.pallas_call(
@@ -224,8 +243,9 @@
         in_specs=[SMEM] * 6 + [VMEM] * 2,
         out_specs=VMEM,
         scratch_shapes=profiles,
+        compiler_params=LIMIT,
         name="spread",
-    )(place, coverage, unit_chan, unit_block, tile_anchor, roots, both, beam)
+    )(place, coverage, unit_chan, blocks, anchors, roots, both, beam)
     parts = lax.all_to_all(images, "chip", 0, 0, tiled=True)
 
     spread = pl.pallas_call(
@@ -233,6 +253,7 @@
         out_shape=shape((TILES_DEV, PIXELS, PIXELS), BF),
         in_specs=[SMEM] * 2 + [VMEM],
         out_specs=VMEM,
+        compiler_params=LIMIT,
         name="gather",
     )(place, coverage, parts)
     share = TILES_DEV * PIXELS // pointings
@@ -244,6 +265,7 @@
         out_shape=shape((pointings, share, PIXELS), BF),
         in_specs=[VMEM],
         out_specs=VMEM,
+        compiler_params=LIMIT,
         name="total",
     )(shares)
     image = lax.all_to_all(repeated, "uv", 0, 0, tiled=True)

time: 131 us -> 116 us (0.89)
  blocking collectives: 85.4 us -> 99.3 us
  starting transfers between devices: 11.3 us -> 1.92 us
  waiting for transfers between devices: 9.78 us -> 1.5 us
  Pallas kernels: 16.5 us -> 9.22 us
  local copies, waits for them, and re-layouts: 6.22 us -> 3.18 us
    all_to_all x0 -> x1, blocking collectives: none -> 18.6 us  [per_device(): tiles = lax.all_to_all(copies, 'chip', 0, 0, tiled=True)]
    all_to_all x1 -> x0, starting transfers between devices: 9.37 us -> none  [per_device(): tiles = lax.all_to_all(copies, 'chip', 0, 0, tiled=True)]
    all_to_all x1 -> x0, waiting for transfers between devices: 8.07 us -> none  [per_device(): tiles = lax.all_to_all(copies, 'chip', 0, 0, tiled=True)]
    all_gather x1, blocking collectives: 5.1 us -> 2.17 us  [per_device(): both = lax.all_gather(turned, 'core', axis=0, tiled=True)]
    pallas_call x1, Pallas kernels: 1.95 us -> 0.1 us  [per_device(): pl.pallas_call(total_kernel, out_shape=shape((pointings, share, PIXELS),...]
    pallas_call x1, Pallas kernels: 4.5 us -> 2.71 us  [per_device(): pl.pallas_call(spread_kernel, out_shape=shape((CHIPS, PIXELS, PIXELS), BF...]
    pallas_call x1, Pallas kernels: 4.39 us -> 2.73 us  [per_device(): pl.pallas_call(combine_kernel, out_shape=(shape((2, PIXELS, PIXELS), F32)...]
    pallas_call x1, Pallas kernels: 2.27 us -> 0.78 us  [per_device(): pl.pallas_call(gather_kernel, out_shape=shape((TILES_DEV, PIXELS, PIXELS)...]
  transfers between devices with their start and end apart: 2 -> 1, of which waited for: 2 -> 1; matrix products, arithmetic and copies ran while one was open for 1% -> 0% of each run, Pallas kernels for 0% -> 0%
where the time goes in v2:
time: 116 us
  blocking collectives  99.3 us (86%)
  Pallas kernels  9.22 us (8%)
  local copies, waits for them, and re-layouts  3.18 us (3%)
  starting transfers between devices  1.92 us (2%)
  waiting for transfers between devices  1.5 us (1%)
    all_to_all x1, blocking collectives, per_device(): shares = lax.all_to_all(spread, 'uv', 0, 0, tiled=True)  35.3 us
    all_to_all x1, blocking collectives, per_device(): image = lax.all_to_all(repeated, 'uv', 0, 0, tiled=True)  24.6 us
    all_to_all x1, blocking collectives, per_device(): parts = lax.all_to_all(images, 'chip', 0, 0, tiled=True)  18.7 us
    all_to_all x1, blocking collectives, per_device(): tiles = lax.all_to_all(copies, 'chip', 0, 0, tiled=True)  18.6 us
    unnamed x21, local copies, waits for them, and re-layouts  3.18 us
    pallas_call x1, Pallas kernels, per_device(): pl.pallas_call(combine_kernel, out_shape=(shape((2, PIXELS, PIXELS), F32)...  2.73 us
    pallas_call x1, Pallas kernels, per_device(): pl.pallas_call(spread_kernel, out_shape=shape((CHIPS, PIXELS, PIXELS), BF...  2.71 us
  transfers between devices with their start and end apart: 1, of which 1 were waited for; matrix products, arithmetic and copies ran while one was open for 0% of the time, Pallas kernels for 0%

profile of v2, /device:TPU:14, one launch (start us, length us, event | category | flops | bytes accessed | tf_op | source)
XLA Modules:
  0.0 115.9 jit_solution(216864685317841845)
XLA Ops:
  0.6 0.0 copy-start.5
  0.6 0.6 copy-done.5
  1.3 0.0 copy-start.1
  1.3 1.0 copy-done.1
  2.3 0.6 copies.1
  3.0 0.0 copy-start
  3.0 0.0 copy-start.6
  3.0 0.0 copy-start.7
  3.0 18.6 %all_to_all.20.tiles = bf16[8,256,256]{2,1,0:T(8,128)(2,1)S(1)} all-to-all(bf16[8,256,256]{2,1,0:T(8,128)(2,1)S(1)} %copies.1), channel_id=1, replica_groups=mesh['chip'=8,'core'=2,'uv'=32] {'chip'}, dimensions={0} | all-to-all | bytes 2097152 | tf_op jit(solution)/shard_map/all_to_all | solution.py:213
  21.6 0.0 copy-start.4
  21.6 0.0 copy-start.8
  21.6 0.0 copy-done
  21.6 0.0 copy-done.6
  21.6 0.0 copy-done.7
  21.6 0.7 copy-done.4
  22.3 0.0 copy-done.8
  22.3 2.7 %combine.1 = (f32[2,256,256]{2,1,0:T(8,128)S(1)}, bf16[2,256,256]{2,1,0:T(8,128)(2,1)S(1)}) custom-call(s32[1]{0:T(128)} %bitcast.place, s32[1,16]{1,0:T(1,128)S(1)} %copy-done.5, s32[1,16]{1,0:T(1,128)S(1)} %copy-done.8, s32[1,2,16]{2,1,0:T(2,128)S(1)} %bitcast.6, s32[2,64]{1,0:T(2,128)S(1)} %bitcast.9, f32[2,64]{1,0:T(2,128)S(1)} %copy-done.7, ...), custom_call_target="tpu_custom_call" | custom-call | tf_op jit(solution)/shard_map/combine/pallas_call | solution.py:215
  25.0 0.0 copy-start.9
  25.1 1.9 %collective-permute-start = (bf16[2,256,256]{2,1,0:T(8,128)(2,1)S(1)}, bf16[2,256,256]{2,1,0:T(8,128)(2,1)S(1)}, u32[]{:S(2)}, u32[]{:S(2)}) collective-permute-start(bf16[2,256,256]{2,1,0:T(8,128)(2,1)S(1)} %get-tuple-element.7), channel_id=1, source_target_pairs={{0,32},{32,0},{1,33},{33,1},{2,34},{34,2},{3,35},{35,3},{4,36},{36... | collective-permute-start | bytes 786440 | tf_op jit(solution)/shard_map/ppermute | solution.py:224
  27.0 1.5 %collective-permute-done.arrived = bf16[2,256,256]{2,1,0:T(8,128)(2,1)S(1)} collective-permute-done((bf16[2,256,256]{2,1,0:T(8,128)(2,1)S(1)}, bf16[2,256,256]{2,1,0:T(8,128)(2,1)S(1)}, u32[]{:S(2)}, u32[]{:S(2)}) %collective-permute-start) | collective-permute-done | bytes 262176 | tf_op jit(solution)/shard_map/ppermute | solution.py:224
  28.5 0.0 copy-done.2
  28.5 0.0 copy-done.3
  28.5 0.0 copy-done.9
  28.5 2.3 %unit.1 = (bf16[1,1,2,256,256]{4,3,2,1,0:T(8,128)(2,1)}, bf16[1,2,256,256]{3,2,1,0:T(8,128)(2,1)S(1)}) custom-call(s32[1]{0:T(128)} %bitcast.place, s32[1,2,16]{2,1,0:T(2,128)S(1)} %bitcast.7, s32[1,16]{1,0:T(1,128)S(1)} %copy-done.9, f32[2,256,256]{2,1,0:T(8,128)S(1)} %get-tuple-element.6.own, bf16[2,256,256]{2,1,0:T(8,128)(2,1)S(1)} %collective-permute-done.arrived, ...), custom_call_target="tpu_custom_call" | custom-call | tf_op jit(solution)/shard_map/unit/pallas_call | solution.py:226
  30.8 2.2 %all_gather.3.turned = bf16[2,2,256,256]{3,2,1,0:T(8,128)(2,1)S(1)} all-gather(bf16[1,2,256,256]{3,2,1,0:T(8,128)(2,1)S(1)} %get-tuple-element.9), channel_id=1, replica_groups=mesh['chip'=8,'core'=2,'uv'=32] {'core'}, dimensions={0}, use_global_device_ids=true | all-gather | bytes 786432 | tf_op jit(solution)/shard_map/all_gather | solution.py:238
  33.0 2.7 %spread.1 = bf16[8,256,256]{2,1,0:T(8,128)(2,1)S(1)} custom-call(s32[1]{0:T(128)} %bitcast.place, s32[1,16]{1,0:T(1,128)S(1)} %copy-done.5, s32[1,16]{1,0:T(1,128)S(1)} %copy-done.8, s32[1,2,16]{2,1,0:T(2,128)S(1)} %bitcast.8, s32[2,64]{1,0:T(2,128)S(1)} %bitcast.10, f32[2,64]{1,0:T(2,128)S(1)} %copy-done.7, bf16[2,2,256,256]{3,2,1,0:T(8,128)(2,1)S(1)} %all_gather.3.turned, ...), custom_call_target="tpu_custom_call" | custom-call | tf_op jit(solution)/shard_map/spread/pallas_call | solution.py:240
  35.7 18.7 %all_to_all.21.parts = bf16[8,256,256]{2,1,0:T(8,128)(2,1)S(1)} all-to-all(bf16[8,256,256]{2,1,0:T(8,128)(2,1)S(1)} %spread.1), channel_id=1, replica_groups=mesh['chip'=8,'core'=2,'uv'=32] {'chip'}, dimensions={0} | all-to-all | bytes 2097152 | tf_op jit(solution)/shard_map/all_to_all | solution.py:249
  54.4 0.8 gather.1
  55.1 35.3 %all_to_all.22.parts = bf16[32,32,256]{2,1,0:T(8,128)(2,1)S(1)} all-to-all(bf16[32,32,256]{2,1,0:T(8,128)(2,1)S(1)} %bitcast.5), channel_id=1, replica_groups=mesh['chip'=8,'core'=2,'uv'=32] {'uv'}, dimensions={0} | all-to-all | bytes 1048576 | tf_op jit(solution)/shard_map/all_to_all | solution.py:261
  90.4 0.1 total.1
  90.5 24.6 %all_to_all.23 = bf16[32,32,256]{2,1,0:T(8,128)(2,1)S(1)} all-to-all(bf16[32,32,256]{2,1,0:T(8,128)(2,1)S(1)} %total.1), channel_id=1, replica_groups=mesh['chip'=8,'core'=2,'uv'=32] {'uv'}, dimensions={0} | all-to-all | bytes 1048576 | tf_op jit(solution)/shard_map/all_to_all | solution.py:271
  115.1 0.8 copy.13
  (2 shorter events, 0.0 us)
Async XLA Ops:
  0.6 0.7 copy-start.5
  1.3 1.0 copy-start.1
  3.0 18.7 %copy-start = (f32[1,4,16,2,256]{4,3,2,1,0:T(2,128)S(1)}, f32[1,4,16,2,256]{4,3,2,1,0:T(2,128)}, u32[]{:S(2)}) copy-start(f32[1,4,16,2,256]{4,3,2,1,0:T(2,128)} %beam.3) | copy-start | bytes 393220
  3.0 18.7 %copy-start.6 = (s32[64,2]{0,1:T(2,128)S(1)}, s32[64,2]{0,1:T(2,128)}, u32[]{:S(2)}) copy-start(s32[64,2]{0,1:T(2,128)} %param.12) | copy-start | bytes 1540
  3.0 18.7 %copy-start.7 = (f32[2,64]{1,0:T(2,128)S(1)}, f32[2,64]{1,0:T(2,128)}, u32[]{:S(2)}) copy-start(f32[2,64]{1,0:T(2,128)} %constant.18.clone.roots) | copy-start | bytes 1540
  21.6 0.7 copy-start.4
  21.6 0.7 copy-start.8
  22.3 6.2 %copy-start.2 = (bf16[1,1,2,256,256]{4,3,2,1,0:T(8,128)(2,1)S(1)}, bf16[1,1,2,256,256]{4,3,2,1,0:T(8,128)(2,1)}, u32[]{:S(2)}) copy-start(bf16[1,1,2,256,256]{4,3,2,1,0:T(8,128)(2,1)} %observed.1) | copy-start | bytes 786436
  22.3 6.2 %copy-start.3 = (bf16[2,256,256]{2,1,0:T(8,128)(2,1)S(1)}, bf16[2,256,256]{2,1,0:T(8,128)(2,1)}, u32[]{:S(2)}) copy-start(bf16[2,256,256]{2,1,0:T(8,128)(2,1)} %constant.19.clone.table) | copy-start | bytes 786436
  25.0 3.4 %copy-start.9 = (s32[1,16]{1,0:T(1,128)S(1)}, s32[1,16]{1,0:T(1,128)}, u32[]{:S(2)}) copy-start(s32[1,16]{1,0:T(1,128)} %masks.1) | copy-start | bytes 196
  25.1 3.4 %collective-permute-start = (bf16[2,256,256]{2,1,0:T(8,128)(2,1)S(1)}, bf16[2,256,256]{2,1,0:T(8,128)(2,1)S(1)}, u32[]{:S(2)}, u32[]{:S(2)}) collective-permute-start(bf16[2,256,256]{2,1,0:T(8,128)(2,1)S(1)} %get-tuple-element.7), channel_id=1, source_target_pairs={{0,32},{32,0},{1,33},{33,1},{2,34},{34,2},{3,35},{35,3},{4,36},{36... | collective-permute-start | bytes 786440 | tf_op jit(solution)/shard_map/ppermute | solution.py:224

commit v3 on v2

v3 whole, which is shorter than its diff:
```python
import math

import jax
import jax.numpy as jnp
import numpy as np
from jax import lax
from jax.experimental import pallas as pl
from jax.experimental.pallas import tpu as pltpu
from jax.sharding import Mesh, PartitionSpec as P

PIXELS = 256
GRID_TILES = 64
TURN = GRID_TILES * PIXELS
TILES_DEV = 4
CHIPS = 8
CORES = 2
UNITS = CHIPS * CORES
ROWS = 16
MARK = 128
BF = jnp.bfloat16
F32 = jnp.float32

LIMIT = pltpu.CompilerParams(vmem_limit_bytes=12 * 1024 * 1024)

SMEM = pl.BlockSpec(memory_space=pltpu.SMEM)
VMEM = pl.BlockSpec(memory_space=pltpu.VMEM)


def dft_matrix():
    counter = np.arange(PIXELS)
    angles = 2.0 * np.pi * (counter[:, None] * counter[None, :] % PIXELS) / PIXELS
    return jnp.asarray(np.stack([np.cos(angles), np.sin(angles)]) / math.sqrt(PIXELS), BF)


def anchor_roots():
    angles = 2.0 * np.pi * np.arange(GRID_TILES) / GRID_TILES
    return jnp.asarray(np.stack([np.cos(angles), np.sin(angles)]), F32)


def dot(left, right):
    return jnp.dot(left, right, preferred_element_type=F32)


def slot_phase(coverage, anchors, blocks, roots, unit, slot):
    tile = coverage[0, slot]
    turns = blocks[0, 0, unit] * anchors[0, tile] + blocks[0, 1, unit] * anchors[1, tile]
    turns = lax.bitwise_and(turns, GRID_TILES - 1)
    return roots[0, turns], roots[1, turns]


def prepare_kernel(
    place, coverage, chans, blocks, anchors, roots, tiles, beam, copies, firsts, seconds, phases
):
    sky = place[0]
    own = tiles[coverage[0, sky] - sky * TILES_DEV]
    for chip in range(CHIPS):
        copies[chip] = own
    core = lax.bitwise_and(sky, 1)
    lines = []
    for e in range(CORES):
        unit = sky - core + e
        channel = chans[0, unit]
        for chip in range(CHIPS):
            line = e * CHIPS + chip
            slot = CORES * chip + core
            pair = beam[0, channel, slot]
            lines.append(pair[0:1])
            seconds[line : line + 1, :] = pair[1:2]
            cosine, sine = slot_phase(coverage, anchors, blocks, roots, unit, slot)
            phases[0, line] = cosine
            phases[1, line] = sine
    firsts[...] = jnp.transpose(jnp.concatenate(lines, axis=0))


def combine_kernel(place, phases, tiles, firsts, seconds, own, other):
    core = lax.bitwise_and(place[0], 1)

    @pl.loop(0, PIXELS // ROWS)
    def step(at):
        rows = pl.ds(pl.multiple_of(at * ROWS, ROWS), ROWS)
        first = firsts[rows, :]
        sums = [[jnp.zeros((ROWS, PIXELS), F32) for _ in range(2)] for _ in range(CORES)]
        for chip in range(CHIPS):
            tile = tiles[chip, rows, :].astype(F32)
            for e in range(CORES):
                line = e * CHIPS + chip
                weighted = tile * seconds[line : line + 1, :] * first[:, line : line + 1]
                sums[e][0] += phases[0, line] * weighted
                sums[e][1] += phases[1, line] * weighted
        for plane in range(2):
            own[plane, rows, :] = jnp.where(core == 0, sums[0][plane], sums[1][plane])
            other[0, plane, rows, :] = jnp.where(core == 0, sums[1][plane], sums[0][plane]).astype(BF)


def twiddles(offset):
    turns = lax.bitwise_and(offset * lax.broadcasted_iota(jnp.int32, (8, PIXELS), 1), TURN - 1)
    angles = turns.astype(F32) * (2.0 * math.pi / TURN)
    return jnp.cos(angles), jnp.sin(angles)


def unit_kernel(place, blocks, masks, own, arrived, observed, table, residual, turned, shift):
    sky = place[0]
    partner = 1 - lax.bitwise_and(sky, 1)
    col_cos, col_sin = twiddles(blocks[0, 1, sky])
    row_cos, row_sin = twiddles(blocks[0, 0, sky])
    row_cos, row_sin = jnp.transpose(row_cos)[:, 0:1], jnp.transpose(row_sin)[:, 0:1]
    col_cos, col_sin = col_cos[0:1], col_sin[0:1]
    shift[0] = row_cos * col_cos - row_sin * col_sin
    shift[1] = row_sin * col_cos + row_cos * col_sin

    sum_re = own[0] + arrived[partner, 0].astype(F32)
    sum_im = own[1] + arrived[partner, 1].astype(F32)
    sky_re = (sum_re * shift[0] - sum_im * shift[1]).astype(BF)
    sky_im = (sum_re * shift[1] + sum_im * shift[0]).astype(BF)
    cosines, sines = table[0], table[1]
    part_re = (dot(sky_re, cosines) - dot(sky_im, sines)).astype(BF)
    part_im = (dot(sky_re, sines) + dot(sky_im, cosines)).astype(BF)
    model_re = dot(cosines, part_re) - dot(sines, part_im)
    model_im = -(dot(sines, part_re) + dot(cosines, part_im))

    occupied = masks[0, sky].astype(F32)
    res_re = (occupied * (observed[0, 0, 0].astype(F32) - model_re)).astype(BF)
    res_im = (occupied * (observed[0, 0, 1].astype(F32) - model_im)).astype(BF)
    residual[0, 0, 0] = res_re
    residual[0, 0, 1] = res_im
    part_re = (dot(cosines, res_re) - dot(sines, res_im)).astype(BF)
    part_im = (dot(sines, res_re) + dot(cosines, res_im)).astype(BF)
    back_re = dot(part_re, cosines) - dot(part_im, sines)
    back_im = dot(part_re, sines) + dot(part_im, cosines)
    turned[0, 0] = (back_re * shift[0] - back_im * shift[1]).astype(BF)
    turned[0, 1] = (back_re * shift[1] + back_im * shift[0]).astype(BF)


def spread_kernel(phases, turned, firsts, seconds, images):
    @pl.loop(0, PIXELS // ROWS)
    def step(at):
        rows = pl.ds(pl.multiple_of(at * ROWS, ROWS), ROWS)
        first = firsts[rows, :]
        planes = [[turned[e, plane, rows, :].astype(F32) for plane in range(2)] for e in range(CORES)]
        for chip in range(CHIPS):
            total = None
            for e in range(CORES):
                line = e * CHIPS + chip
                part = phases[0, line] * planes[e][0] - phases[1, line] * planes[e][1]
                part = part * seconds[line : line + 1, :] * first[:, line : line + 1]
                total = part if total is None else total + part
            images[chip, rows, :] = total.astype(BF)


def gather_kernel(place, coverage, parts, shares):
    sky = place[0]
    position = (coverage[0, sky] - sky * TILES_DEV).astype(F32)
    pointings, share = shares.shape[0], shares.shape[1]
    total = parts[0].astype(F32)
    for chip in range(1, CHIPS):
        total += parts[chip].astype(F32)
    shares[:, :, 0:PIXELS] = total.reshape(pointings, share, PIXELS).astype(BF)
    shares[:, :, PIXELS:] = jnp.full((pointings, share, MARK), position, F32).astype(BF)


def total_kernel(shares, repeated):
    pointings, share = shares.shape[0], shares.shape[1]
    totals = [jnp.zeros((share, PIXELS), F32) for _ in range(TILES_DEV)]
    for p in range(pointings):
        values = shares[p, :, 0:PIXELS].astype(F32)
        mark = shares[p, :, PIXELS:].astype(F32)
        mark = jnp.concatenate([mark] * (PIXELS // MARK), axis=1)
        for position in range(TILES_DEV):
            totals[position] += jnp.where(mark == position, values, 0.0)
    totals = [total.astype(BF) for total in totals]
    for p in range(pointings):
        for position in range(TILES_DEV):
            repeated[p, position] = totals[position]


def shape(dims, kind):
    return jax.ShapeDtypeStruct(dims, kind)


def per_device(
    sky_model, beam, tile_anchor, coverage, unit_chan, unit_block, unit_occupied_mask, observed
):
    chip_core = lax.axis_index("chip") * CORES + lax.axis_index("core")
    place = chip_core.astype(jnp.int32).reshape(1)
    pointings = lax.axis_size("uv")
    anchors = tile_anchor.T
    blocks = jnp.swapaxes(unit_block, 1, 2)

    copies, firsts, seconds, phases = pl.pallas_call(
        prepare_kernel,
        out_shape=(
            shape((CHIPS, PIXELS, PIXELS), BF),
            shape((PIXELS, UNITS), F32),
            shape((UNITS, PIXELS), F32),
            shape((2, UNITS), F32),
        ),
        in_specs=[SMEM] * 6 + [VMEM] * 2,
        out_specs=(VMEM, VMEM, VMEM, SMEM),
        compiler_params=LIMIT,
        name="prepare",
    )(place, coverage, unit_chan, blocks, anchors, anchor_roots(), sky_model, beam)
    tiles = lax.all_to_all(copies, "chip", 0, 0, tiled=True)

    own, other = pl.pallas_call(
        combine_kernel,
        out_shape=(shape((2, PIXELS, PIXELS), F32), shape((1, 2, PIXELS, PIXELS), BF)),
        in_specs=[SMEM] * 2 + [VMEM] * 3,
        out_specs=(VMEM, VMEM),
        compiler_params=LIMIT,
        name="combine",
    )(place, phases, tiles, firsts, seconds)
    arrived = lax.all_gather(other, "core", axis=0, tiled=True)

    residual, turned = pl.pallas_call(
        unit_kernel,
        out_shape=(
            shape((1, 1, 2, PIXELS, PIXELS), BF),
            shape((1, 2, PIXELS, PIXELS), BF),
        ),
        in_specs=[SMEM] * 3 + [VMEM] * 4,
        out_specs=(VMEM, VMEM),
        scratch_shapes=[pltpu.VMEM((2, PIXELS, PIXELS), F32)],
        compiler_params=LIMIT,
        name="unit",
    )(place, blocks, unit_occupied_mask, own, arrived, observed, dft_matrix())
    both = lax.all_gather(turned, "core", axis=0, tiled=True)

    images = pl.pallas_call(
        spread_kernel,
        out_shape=shape((CHIPS, PIXELS, PIXELS), BF),
        in_specs=[SMEM] + [VMEM] * 3,
        out_specs=VMEM,
        compiler_params=LIMIT,
        name="spread",
    )(phases, both, firsts, seconds)
    parts = lax.all_to_all(images, "chip", 0, 0, tiled=True)

    share = PIXELS // pointings
    shares = pl.pallas_call(
        gather_kernel,
        out_shape=shape((pointings, share, PIXELS + MARK), BF),
        in_specs=[SMEM] * 2 + [VMEM],
        out_specs=VMEM,
        compiler_params=LIMIT,
        name="gather",
    )(place, coverage, parts)
    shares = lax.all_to_all(shares, "uv", 0, 0, tiled=True)

    repeated = pl.pallas_call(
        total_kernel,
        out_shape=shape((pointings, TILES_DEV, share, PIXELS), BF),
        in_specs=[VMEM],
        out_specs=VMEM,
        compiler_params=LIMIT,
        name="total",
    )(shares)
    image = lax.all_to_all(repeated, "uv", 0, 0, tiled=True)
    return residual, jnp.swapaxes(image, 0, 1).reshape(TILES_DEV, PIXELS, PIXELS)


def solution(mesh):
    pointings = mesh.shape["uv"]
    fine = Mesh(mesh.devices.reshape(CHIPS, CORES, pointings), ("chip", "core", "uv"))
    sky = ("chip", "core")
    return jax.shard_map(
        per_device,
        mesh=fine,
        in_specs=(
            P(sky, None, None),
            P("uv", None, None, None, None),
            P(),
            P("uv", None),
            P("uv", None),
            P("uv", None, None),
            P("uv", None),
            P("uv", sky, None, None, None),
        ),
        out_specs=(P("uv", sky, None, None, None), P(sky, None, None)),
        check_vma=False,
    )
```

time: 116 us -> 108 us (0.931)
  the two profiles are of different devices: /device:TPU:14 before, /device:TPU:12 now
where the time goes in v3:
time: 108 us
  blocking collectives  93.3 us (86%)
  Pallas kernels  9.42 us (9%)
  local copies, waits for them, and re-layouts  4.12 us (4%)
    all_to_all x1, blocking collectives, per_device(): shares = lax.all_to_all(shares, 'uv', 0, 0, tiled=True)  28.1 us
    all_to_all x1, blocking collectives, per_device(): image = lax.all_to_all(repeated, 'uv', 0, 0, tiled=True)  24.3 us
    all_to_all x1, blocking collectives, per_device(): parts = lax.all_to_all(images, 'chip', 0, 0, tiled=True)  18.6 us
    all_to_all x1, blocking collectives, per_device(): tiles = lax.all_to_all(copies, 'chip', 0, 0, tiled=True)  17.9 us
    unnamed x20, local copies, waits for them, and re-layouts  3.3 us
    pallas_call x1, Pallas kernels, per_device(): pl.pallas_call(combine_kernel, out_shape=(shape((2, PIXELS, PIXELS), F32)...  2.54 us
    pallas_call x1, Pallas kernels, per_device(): pl.pallas_call(spread_kernel, out_shape=shape((CHIPS, PIXELS, PIXELS), BF...  2.46 us
    all_gather x1, blocking collectives, per_device(): arrived = lax.all_gather(other, 'core', axis=0, tiled=True)  2.31 us

profile of v3, /device:TPU:12, one launch (start us, length us, event | category | flops | bytes accessed | tf_op | source)
XLA Modules:
  0.0 107.6 jit_solution(11732118994521207551)
XLA Ops:
  0.6 0.0 copy-start.9
  0.6 0.0 copy-start.6
  0.7 0.0 copy-start.7
  0.7 0.0 copy-start.4
  0.7 0.0 copy-start.5
  0.7 0.6 copy-done.9
  1.3 0.0 copy-done.6
  1.3 0.0 copy-done.7
  1.4 0.0 copy-done.4
  1.4 0.0 copy-done.5
  1.4 0.0 copy-start
  1.4 1.0 copy-done
  2.4 0.0 copy-start.3
  2.4 0.9 copy-done.3
  3.3 1.3 %prepare.1 = (bf16[8,256,256]{2,1,0:T(8,128)(2,1)S(1)}, f32[256,16]{1,0:T(8,128)S(1)}, f32[16,256]{1,0:T(8,128)S(1)}, f32[2,16]{1,0:T(2,128)S(1)}) custom-call(s32[1]{0:T(128)} %bitcast.place, s32[1,16]{1,0:T(1,128)S(1)} %copy-done.5, s32[1,16]{1,0:T(1,128)S(1)} %copy-done.9, s32[1,2,16]{2,1,0:T(2,128)S(1)} %bitcast.8, s32[2,64]{1,0:T(2,128)S(1)} %bitcast.10, ...), custom_call_target="tpu_custom_call" | custom-call | tf_op jit(solution)/shard_map/prepare/pallas_call | solution.py:189
  4.6 17.9 %all_to_all.20.tiles = bf16[8,256,256]{2,1,0:T(8,128)(2,1)S(1)} all-to-all(bf16[8,256,256]{2,1,0:T(8,128)(2,1)S(1)} %get-tuple-element.11), channel_id=1, replica_groups=mesh['chip'=8,'core'=2,'uv'=32] {'chip'}, dimensions={0} | all-to-all | bytes 2097152 | tf_op jit(solution)/shard_map/all_to_all | solution.py:202
  22.5 2.5 %combine.1 = (f32[2,256,256]{2,1,0:T(8,128)S(1)}, bf16[1,2,256,256]{3,2,1,0:T(8,128)(2,1)S(1)}) custom-call(s32[1]{0:T(128)} %bitcast.place, f32[2,16]{1,0:T(2,128)S(1)} %get-tuple-element.10.phases, bf16[8,256,256]{2,1,0:T(8,128)(2,1)S(1)} %all_to_all.20.tiles, f32[256,16]{1,0:T(8,128)S(1)} %get-tuple-element.12.firsts, f32[16,256]{1,0:T(8,128)S(1)} %get-tuple-element.13.seconds), custom_call_target="tpu_custom_call" | custom-call | tf_op jit(solution)/shard_map/combine/pallas_call | solution.py:204
  25.1 0.0 copy-start.1
  25.1 0.0 copy-start.2
  25.1 2.3 %all_gather.6.arrived = bf16[2,2,256,256]{3,2,1,0:T(8,128)(2,1)S(1)} all-gather(bf16[1,2,256,256]{3,2,1,0:T(8,128)(2,1)S(1)} %get-tuple-element.15), channel_id=1, replica_groups=mesh['chip'=8,'core'=2,'uv'=32] {'core'}, dimensions={0}, use_global_device_ids=true | all-gather | bytes 786432 | tf_op jit(solution)/shard_map/all_gather | solution.py:212
  27.4 0.0 copy-done.1
  27.4 0.0 copy-done.2
  27.4 0.6 copy-done.8
  28.1 2.3 %unit.1 = (bf16[1,1,2,256,256]{4,3,2,1,0:T(8,128)(2,1)}, bf16[1,2,256,256]{3,2,1,0:T(8,128)(2,1)S(1)}) custom-call(s32[1]{0:T(128)} %bitcast.place, s32[1,2,16]{2,1,0:T(2,128)S(1)} %bitcast.9, s32[1,16]{1,0:T(1,128)S(1)} %copy-done.8, f32[2,256,256]{2,1,0:T(8,128)S(1)} %get-tuple-element.14.own, bf16[2,2,256,256]{3,2,1,0:T(8,128)(2,1)S(1)} %all_gather.6.arrived, ...), custom_call_target="tpu_custom_call" | custom-call | tf_op jit(solution)/shard_map/unit/pallas_call | solution.py:214
  30.4 2.2 %all_gather.7.turned = bf16[2,2,256,256]{3,2,1,0:T(8,128)(2,1)S(1)} all-gather(bf16[1,2,256,256]{3,2,1,0:T(8,128)(2,1)S(1)} %get-tuple-element.17), channel_id=1, replica_groups=mesh['chip'=8,'core'=2,'uv'=32] {'core'}, dimensions={0}, use_global_device_ids=true | all-gather | bytes 786432 | tf_op jit(solution)/shard_map/all_gather | solution.py:226
  32.5 2.5 %spread.1 = bf16[8,256,256]{2,1,0:T(8,128)(2,1)S(1)} custom-call(f32[2,16]{1,0:T(2,128)S(1)} %get-tuple-element.10.phases, bf16[2,2,256,256]{3,2,1,0:T(8,128)(2,1)S(1)} %all_gather.7.turned, f32[256,16]{1,0:T(8,128)S(1)} %get-tuple-element.12.firsts, f32[16,256]{1,0:T(8,128)S(1)} %get-tuple-element.13.seconds), custom_call_target="tpu_custom_call" | custom-call | tf_op jit(solution)/shard_map/spread/pallas_call | solution.py:228
  35.0 18.6 %all_to_all.21.parts = bf16[8,256,256]{2,1,0:T(8,128)(2,1)S(1)} all-to-all(bf16[8,256,256]{2,1,0:T(8,128)(2,1)S(1)} %spread.1), channel_id=1, replica_groups=mesh['chip'=8,'core'=2,'uv'=32] {'chip'}, dimensions={0} | all-to-all | bytes 2097152 | tf_op jit(solution)/shard_map/all_to_all | solution.py:236
  53.6 0.7 gather.1
  54.3 28.1 %all_to_all.22.shares = bf16[32,8,384]{2,1,0:T(8,128)(2,1)S(1)} all-to-all(bf16[32,8,384]{2,1,0:T(8,128)(2,1)S(1)} %gather.1), channel_id=1, replica_groups=mesh['chip'=8,'core'=2,'uv'=32] {'uv'}, dimensions={0} | all-to-all | bytes 393216 | tf_op jit(solution)/shard_map/all_to_all | solution.py:247
  82.4 0.1 total.1
  82.5 24.3 %all_to_all.23 = bf16[32,4,8,256]{3,2,1,0:T(8,128)(2,1)S(1)} all-to-all(bf16[32,4,8,256]{3,2,1,0:T(8,128)(2,1)S(1)} %total.1), channel_id=1, replica_groups=mesh['chip'=8,'core'=2,'uv'=32] {'uv'}, dimensions={0} | all-to-all | bytes 1048576 | tf_op jit(solution)/shard_map/all_to_all | solution.py:257
  106.8 0.8 copy_bitcast_fusion
  (1 shorter events, 0.0 us)
Async XLA Ops:
  0.6 0.7 copy-start.9
  0.6 0.7 copy-start.6
  0.7 0.7 copy-start.7
  0.7 0.7 copy-start.4
  0.7 0.7 copy-start.5
  1.4 1.0 copy-start
  2.4 0.9 copy-start.3
  25.1 2.3 %copy-start.1 = (bf16[1,1,2,256,256]{4,3,2,1,0:T(8,128)(2,1)S(1)}, bf16[1,1,2,256,256]{4,3,2,1,0:T(8,128)(2,1)}, u32[]{:S(2)}) copy-start(bf16[1,1,2,256,256]{4,3,2,1,0:T(8,128)(2,1)} %observed.1) | copy-start | bytes 786436
  25.1 2.3 %copy-start.2 = (bf16[2,256,256]{2,1,0:T(8,128)(2,1)S(1)}, bf16[2,256,256]{2,1,0:T(8,128)(2,1)}, u32[]{:S(2)}) copy-start(bf16[2,256,256]{2,1,0:T(8,128)(2,1)} %constant.19.clone.table) | copy-start | bytes 786436
  27.4 0.7 copy-start.8

commit v4 on v3

--- a/solution.py
+++ b/solution.py
@@ -15,8 +15,12 @@
 CHIPS = 8
 CORES = 2
 UNITS = CHIPS * CORES
-ROWS = 16
+ROWS = 32
+UNROLL = 2
 MARK = 128
+COSINE = UNITS
+SINE = UNITS + 8
+LINES = UNITS + 16
 BF = jnp.bfloat16
 F32 = jnp.float32
 
@@ -48,14 +52,30 @@
     return roots[0, turns], roots[1, turns]
 
 
+def copies_kernel(place, coverage, tiles, copies, own, fetched, stored):
+    sky = place[0]
+    fetch = pltpu.make_async_copy(tiles.at[coverage[0, sky] - sky * TILES_DEV], own, fetched)
+    fetch.start()
+    fetch.wait()
+    stores = [pltpu.make_async_copy(own, copies.at[chip], stored.at[chip]) for chip in range(CHIPS)]
+    for store in stores:
+        store.start()
+    for store in stores:
+        store.wait()
+
+
+def twiddles(offset):
+    turns = lax.bitwise_and(offset * lax.broadcasted_iota(jnp.int32, (8, PIXELS), 1), TURN - 1)
+    angles = turns.astype(F32) * (2.0 * math.pi / TURN)
+    return jnp.concatenate([jnp.cos(angles), jnp.sin(angles)], axis=0)
+
+
 def prepare_kernel(
-    place, coverage, chans, blocks, anchors, roots, tiles, beam, copies, firsts, seconds, phases
+    place, coverage, chans, blocks, masks, anchors, roots, beam, firsts, seconds, phases, occupied
 ):
     sky = place[0]
-    own = tiles[coverage[0, sky] - sky * TILES_DEV]
-    for chip in range(CHIPS):
-        copies[chip] = own
     core = lax.bitwise_and(sky, 1)
+    occupied[0] = masks[0, sky].astype(F32)
     lines = []
     for e in range(CORES):
         unit = sky - core + e
@@ -69,13 +89,23 @@
             cosine, sine = slot_phase(coverage, anchors, blocks, roots, unit, slot)
             phases[0, line] = cosine
             phases[1, line] = sine
-    firsts[...] = jnp.transpose(jnp.concatenate(lines, axis=0))
-
-
-def combine_kernel(place, phases, tiles, firsts, seconds, own, other):
+    seconds[UNITS:, :] = twiddles(blocks[0, 1, sky])
+    firsts[...] = jnp.transpose(jnp.concatenate(lines + [twiddles(blocks[0, 0, sky])], axis=0))
+
+
+def combine_kernel(
+    place, phases, tiles, firsts, seconds, observed, table,
+    own, other, weights, observed_near, table_near, near,
+):
     core = lax.bitwise_and(place[0], 1)
-
-    @pl.loop(0, PIXELS // ROWS)
+    fetches = (
+        pltpu.make_async_copy(observed, observed_near, near.at[0]),
+        pltpu.make_async_copy(table, table_near, near.at[1]),
+    )
+    for fetch in fetches:
+        fetch.start()
+
+    @pl.loop(0, PIXELS // ROWS, unroll=UNROLL)
     def step(at):
         rows = pl.ds(pl.multiple_of(at * ROWS, ROWS), ROWS)
         first = firsts[rows, :]
@@ -84,30 +114,25 @@
             tile = tiles[chip, rows, :].astype(F32)
             for e in range(CORES):
                 line = e * CHIPS + chip
-                weighted = tile * seconds[line : line + 1, :] * first[:, line : line + 1]
-                sums[e][0] += phases[0, line] * weighted
-                sums[e][1] += phases[1, line] * weighted
+                shaped = first[:, line : line + 1] * seconds[line : line + 1, :]
+                for plane in range(2):
+                    weight = phases[plane, line] * shaped
+                    weights[plane, line, rows, :] = weight
+                    sums[e][plane] += tile * weight
         for plane in range(2):
             own[plane, rows, :] = jnp.where(core == 0, sums[0][plane], sums[1][plane])
             other[0, plane, rows, :] = jnp.where(core == 0, sums[1][plane], sums[0][plane]).astype(BF)
 
-
-def twiddles(offset):
-    turns = lax.bitwise_and(offset * lax.broadcasted_iota(jnp.int32, (8, PIXELS), 1), TURN - 1)
-    angles = turns.astype(F32) * (2.0 * math.pi / TURN)
-    return jnp.cos(angles), jnp.sin(angles)
-
-
-def unit_kernel(place, blocks, masks, own, arrived, observed, table, residual, turned, shift):
-    sky = place[0]
-    partner = 1 - lax.bitwise_and(sky, 1)
-    col_cos, col_sin = twiddles(blocks[0, 1, sky])
-    row_cos, row_sin = twiddles(blocks[0, 0, sky])
-    row_cos, row_sin = jnp.transpose(row_cos)[:, 0:1], jnp.transpose(row_sin)[:, 0:1]
-    col_cos, col_sin = col_cos[0:1], col_sin[0:1]
+    for fetch in fetches:
+        fetch.wait()
+
+
+def unit_kernel(place, occupied, own, arrived, observed, table, firsts, seconds, residual, turned, shift):
+    partner = 1 - lax.bitwise_and(place[0], 1)
+    row_cos, row_sin = firsts[:, COSINE : COSINE + 1], firsts[:, SINE : SINE + 1]
+    col_cos, col_sin = seconds[COSINE : COSINE + 1, :], seconds[SINE : SINE + 1, :]
     shift[0] = row_cos * col_cos - row_sin * col_sin
     shift[1] = row_sin * col_cos + row_cos * col_sin
-
     sum_re = own[0] + arrived[partner, 0].astype(F32)
     sum_im = own[1] + arrived[partner, 1].astype(F32)
     sky_re = (sum_re * shift[0] - sum_im * shift[1]).astype(BF)
@@ -118,9 +143,8 @@
     model_re = dot(cosines, part_re) - dot(sines, part_im)
     model_im = -(dot(sines, part_re) + dot(cosines, part_im))
 
-    occupied = masks[0, sky].astype(F32)
-    res_re = (occupied * (observed[0, 0, 0].astype(F32) - model_re)).astype(BF)
-    res_im = (occupied * (observed[0, 0, 1].astype(F32) - model_im)).astype(BF)
+    res_re = (occupied[0] * (observed[0, 0, 0].astype(F32) - model_re)).astype(BF)
+    res_im = (occupied[0] * (observed[0, 0, 1].astype(F32) - model_im)).astype(BF)
     residual[0, 0, 0] = res_re
     residual[0, 0, 1] = res_im
     part_re = (dot(cosines, res_re) - dot(sines, res_im)).astype(BF)
@@ -131,18 +155,16 @@
     turned[0, 1] = (back_re * shift[1] + back_im * shift[0]).astype(BF)
 
 
-def spread_kernel(phases, turned, firsts, seconds, images):
-    @pl.loop(0, PIXELS // ROWS)
+def spread_kernel(turned, weights, images):
+    @pl.loop(0, PIXELS // ROWS, unroll=UNROLL)
     def step(at):
         rows = pl.ds(pl.multiple_of(at * ROWS, ROWS), ROWS)
-        first = firsts[rows, :]
         planes = [[turned[e, plane, rows, :].astype(F32) for plane in range(2)] for e in range(CORES)]
         for chip in range(CHIPS):
             total = None
             for e in range(CORES):
                 line = e * CHIPS + chip
-                part = phases[0, line] * planes[e][0] - phases[1, line] * planes[e][1]
-                part = part * seconds[line : line + 1, :] * first[:, line : line + 1]
+                part = planes[e][0] * weights[0, line, rows, :] - planes[e][1] * weights[1, line, rows, :]
                 total = part if total is None else total + part
             images[chip, rows, :] = total.astype(BF)
 
@@ -186,29 +208,50 @@
     anchors = tile_anchor.T
     blocks = jnp.swapaxes(unit_block, 1, 2)
 
-    copies, firsts, seconds, phases = pl.pallas_call(
+    copies = pl.pallas_call(
+        copies_kernel,
+        out_shape=shape((CHIPS, PIXELS, PIXELS), BF),
+        in_specs=[SMEM] * 2 + [pl.BlockSpec(memory_space=pl.ANY)],
+        out_specs=pl.BlockSpec(memory_space=pl.ANY),
+        scratch_shapes=[
+            pltpu.VMEM((PIXELS, PIXELS), BF),
+            pltpu.SemaphoreType.DMA,
+            pltpu.SemaphoreType.DMA((CHIPS,)),
+        ],
+        name="copies",
+    )(place, coverage, sky_model)
+    tiles = lax.all_to_all(copies, "chip", 0, 0, tiled=True)
+
+    firsts, seconds, phases, occupied = pl.pallas_call(
         prepare_kernel,
         out_shape=(
-            shape((CHIPS, PIXELS, PIXELS), BF),
-            shape((PIXELS, UNITS), F32),
-            shape((UNITS, PIXELS), F32),
+            shape((PIXELS, LINES), F32),
+            shape((LINES, PIXELS), F32),
             shape((2, UNITS), F32),
+            shape((1,), F32),
         ),
-        in_specs=[SMEM] * 6 + [VMEM] * 2,
-        out_specs=(VMEM, VMEM, VMEM, SMEM),
+        in_specs=[SMEM] * 7 + [VMEM],
+        out_specs=(VMEM, VMEM, SMEM, SMEM),
         compiler_params=LIMIT,
         name="prepare",
-    )(place, coverage, unit_chan, blocks, anchors, anchor_roots(), sky_model, beam)
-    tiles = lax.all_to_all(copies, "chip", 0, 0, tiled=True)
-
-    own, other = pl.pallas_call(
+    )(place, coverage, unit_chan, blocks, unit_occupied_mask, anchors, anchor_roots(), beam)
+
+    far = pltpu.with_memory_space_constraint
+    own, other, weights, observed_near, table_near = pl.pallas_call(
         combine_kernel,
-        out_shape=(shape((2, PIXELS, PIXELS), F32), shape((1, 2, PIXELS, PIXELS), BF)),
-        in_specs=[SMEM] * 2 + [VMEM] * 3,
-        out_specs=(VMEM, VMEM),
+        out_shape=(
+            shape((2, PIXELS, PIXELS), F32),
+            shape((1, 2, PIXELS, PIXELS), BF),
+            shape((2, UNITS, PIXELS, PIXELS), F32),
+            shape((1, 1, 2, PIXELS, PIXELS), BF),
+            shape((2, PIXELS, PIXELS), BF),
+        ),
+        in_specs=[SMEM] * 2 + [VMEM] * 3 + [pl.BlockSpec(memory_space=pltpu.HBM)] * 2,
+        out_specs=(VMEM,) * 5,
+        scratch_shapes=[pltpu.SemaphoreType.DMA((2,))],
         compiler_params=LIMIT,
         name="combine",
-    )(place, phases, tiles, firsts, seconds)
+    )(place, phases, tiles, firsts, seconds, far(observed, pltpu.HBM), far(dft_matrix(), pltpu.HBM))
     arrived = lax.all_gather(other, "core", axis=0, tiled=True)
 
     residual, turned = pl.pallas_call(
@@ -217,22 +260,22 @@
             shape((1, 1, 2, PIXELS, PIXELS), BF),
             shape((1, 2, PIXELS, PIXELS), BF),
         ),
-        in_specs=[SMEM] * 3 + [VMEM] * 4,
+        in_specs=[SMEM] * 2 + [VMEM] * 6,
         out_specs=(VMEM, VMEM),
         scratch_shapes=[pltpu.VMEM((2, PIXELS, PIXELS), F32)],
         compiler_params=LIMIT,
         name="unit",
-    )(place, blocks, unit_occupied_mask, own, arrived, observed, dft_matrix())
+    )(place, occupied, own, arrived, observed_near, table_near, firsts, seconds)
     both = lax.all_gather(turned, "core", axis=0, tiled=True)
 
     images = pl.pallas_call(
         spread_kernel,
         out_shape=shape((CHIPS, PIXELS, PIXELS), BF),
-        in_specs=[SMEM] + [VMEM] * 3,
+        in_specs=[VMEM] * 2,
         out_specs=VMEM,
         compiler_params=LIMIT,
         name="spread",
-    )(phases, both, firsts, seconds)
+    )(both, weights)
     parts = lax.all_to_all(images, "chip", 0, 0, tiled=True)
 
     share = PIXELS // pointings

time: 108 us -> 103 us (0.954)
  the two profiles are of different devices: /device:TPU:12 before, /device:TPU:10 now
where the time goes in v4:
time: 103 us; the launch traced here: 102 us
  blocking collectives  72.7 us (71%)
  Pallas kernels  9.86 us (10%)
  starting transfers between devices  9.29 us (9%)
  local copies, waits for them, and re-layouts  5.73 us (6%)
  waiting for transfers between devices  3.84 us (4%)
    all_to_all x1, blocking collectives, per_device(): shares = lax.all_to_all(shares, 'uv', 0, 0, tiled=True)  27.6 us
    all_to_all x1, blocking collectives, per_device(): image = lax.all_to_all(repeated, 'uv', 0, 0, tiled=True)  22.2 us
    all_to_all x1, blocking collectives, per_device(): parts = lax.all_to_all(images, 'chip', 0, 0, tiled=True)  18.5 us
    all_to_all x1, starting transfers between devices, per_device(): tiles = lax.all_to_all(copies, 'chip', 0, 0, tiled=True)  9.29 us
    unnamed x16, local copies, waits for them, and re-layouts  4.91 us
    all_to_all x1, waiting for transfers between devices, per_device(): tiles = lax.all_to_all(copies, 'chip', 0, 0, tiled=True)  3.84 us
    pallas_call x1, Pallas kernels, per_device(): pl.pallas_call(copies_kernel, out_shape=shape((CHIPS, PIXELS, PIXELS), BF...  2.62 us
    pallas_call x1, Pallas kernels, per_device(): pl.pallas_call(unit_kernel, out_shape=(shape((1, 1, 2, PIXELS, PIXELS), B...  2.19 us
  transfers between devices with their start and end apart: 1, of which 1 were waited for; matrix products, arithmetic and copies ran while one was open for 0% of the time, Pallas kernels for 1%

profile of v4, /device:TPU:10, one launch (start us, length us, event | category | flops | bytes accessed | tf_op | source)
XLA Modules:
  0.0 102.1 jit_solution(4605944664992054662)
XLA Ops:
  0.6 2.6 %copies.1 = bf16[8,256,256]{2,1,0:T(8,128)(2,1)} custom-call(s32[1]{0:T(128)} %bitcast.place, s32[1,16]{1,0:T(1,128)} %coverage.5, bf16[4,256,256]{2,1,0:T(8,128)(2,1)} %tiles.1), custom_call_target="tpu_custom_call" | custom-call | tf_op jit(solution)/shard_map/copies/pallas_call | solution.py:211
  3.3 9.3 %all-to-all-start = ((bf16[8,256,256]{2,1,0:T(8,128)(2,1)}), bf16[8,256,256]{2,1,0:T(8,128)(2,1)S(1)}, u32[]{:S(2)}, u32[]{:S(2)}) async-start(bf16[8,256,256]{2,1,0:T(8,128)(2,1)} %copies.1), calls=%async_computation | async-start | bytes 2097152 | tf_op jit(solution)/shard_map/all_to_all | solution.py:223
  12.6 0.0 copy-start
  12.6 0.9 copy-done
  13.5 0.0 copy-start.1
  13.5 0.7 copy-done.1
  14.1 0.0 copy-start.3
  14.1 0.7 copy-done.3
  14.8 0.0 copy-start.4
  14.8 0.7 copy-done.4
  15.5 0.0 copy-start.5
  15.5 0.7 copy-done.5
  16.2 0.0 copy-start.6
  16.2 0.7 copy-done.6
  16.8 0.0 copy-start.7
  16.8 0.7 copy-done.7
  17.5 1.3 %prepare.1 = (f32[256,32]{1,0:T(8,128)S(1)}, f32[32,256]{1,0:T(8,128)S(1)}, f32[2,16]{1,0:T(2,128)S(1)}, f32[1]{0:T(128)}) custom-call(s32[1]{0:T(128)} %bitcast.place, s32[1,16]{1,0:T(1,128)S(1)} %copy-done.1, s32[1,16]{1,0:T(1,128)S(1)} %copy-done.6, s32[1,2,16]{2,1,0:T(2,128)S(1)} %bitcast.8, s32[1,16]{1,0:T(1,128)S(1)} %copy-done.7, ...), custom_call_target="tpu_custom_call" | custom-call | tf_op jit(solution)/shard_map/prepare/pallas_call | solution.py:225
  18.8 3.8 %all-to-all-done.tiles = bf16[8,256,256]{2,1,0:T(8,128)(2,1)S(1)} async-done(((bf16[8,256,256]{2,1,0:T(8,128)(2,1)}), bf16[8,256,256]{2,1,0:T(8,128)(2,1)S(1)}, u32[]{:S(2)}, u32[]{:S(2)}) %all-to-all-start) | async-done | bytes 1048608 | tf_op jit(solution)/shard_map/all_to_all | solution.py:223
  22.6 0.0 copy-start.2
  22.6 2.1 %combine.1 = (f32[2,256,256]{2,1,0:T(8,128)S(1)}, bf16[1,2,256,256]{3,2,1,0:T(8,128)(2,1)S(1)}, f32[2,16,256,256]{3,2,1,0:T(8,128)S(1)}, bf16[1,1,2,256,256]{4,3...) custom-call(s32[1]{0:T(128)} %bitcast.place, f32[2,16]{1,0:T(2,128)S(1)} %get-tuple-element.14.phases, ...), custom_call_target="tpu_custom_call" | custom-call | tf_op jit(solution)/shard_map/combine/pallas_call | solution.py:240
  24.8 2.2 %all_gather.6.arrived = bf16[2,2,256,256]{3,2,1,0:T(8,128)(2,1)S(1)} all-gather(bf16[1,2,256,256]{3,2,1,0:T(8,128)(2,1)S(1)} %get-tuple-element.18), channel_id=1, replica_groups=mesh['chip'=8,'core'=2,'uv'=32] {'core'}, dimensions={0}, use_global_device_ids=true | all-gather | bytes 786432 | tf_op jit(solution)/shard_map/all_gather | solution.py:255
  27.0 2.2 %unit.1 = (bf16[1,1,2,256,256]{4,3,2,1,0:T(8,128)(2,1)}, bf16[1,2,256,256]{3,2,1,0:T(8,128)(2,1)S(1)}) custom-call(s32[1]{0:T(128)} %bitcast.place, f32[1]{0:T(128)} %get-tuple-element.13.occupied, f32[2,256,256]{2,1,0:T(8,128)S(1)} %get-tuple-element.17.own, bf16[2,2,256,256]{3,2,1,0:T(8,128)(2,1)S(1)} %all_gather.6.arrived, ...), custom_call_target="tpu_custom_call" | custom-call | tf_op jit(solution)/shard_map/unit/pallas_call | solution.py:257
  29.2 2.2 %all_gather.7.turned = bf16[2,2,256,256]{3,2,1,0:T(8,128)(2,1)S(1)} all-gather(bf16[1,2,256,256]{3,2,1,0:T(8,128)(2,1)S(1)} %get-tuple-element.22), channel_id=1, replica_groups=mesh['chip'=8,'core'=2,'uv'=32] {'core'}, dimensions={0}, use_global_device_ids=true | all-gather | bytes 786432 | tf_op jit(solution)/shard_map/all_gather | solution.py:269
  31.3 0.8 spread.1
  32.1 18.5 %all_to_all.20.parts = bf16[8,256,256]{2,1,0:T(8,128)(2,1)S(1)} all-to-all(bf16[8,256,256]{2,1,0:T(8,128)(2,1)S(1)} %spread.1), channel_id=1, replica_groups=mesh['chip'=8,'core'=2,'uv'=32] {'chip'}, dimensions={0} | all-to-all | bytes 2097152 | tf_op jit(solution)/shard_map/all_to_all | solution.py:279
  50.6 0.0 copy-done.2
  50.6 0.7 gather.1
  51.3 27.6 %all_to_all.21.shares = bf16[32,8,384]{2,1,0:T(8,128)(2,1)S(1)} all-to-all(bf16[32,8,384]{2,1,0:T(8,128)(2,1)S(1)} %gather.1), channel_id=1, replica_groups=mesh['chip'=8,'core'=2,'uv'=32] {'uv'}, dimensions={0} | all-to-all | bytes 393216 | tf_op jit(solution)/shard_map/all_to_all | solution.py:290
  79.0 0.1 total.1
  79.1 22.2 %all_to_all.22 = bf16[32,4,8,256]{3,2,1,0:T(8,128)(2,1)S(1)} all-to-all(bf16[32,4,8,256]{3,2,1,0:T(8,128)(2,1)S(1)} %total.1), channel_id=1, replica_groups=mesh['chip'=8,'core'=2,'uv'=32] {'uv'}, dimensions={0} | all-to-all | bytes 1048576 | tf_op jit(solution)/shard_map/all_to_all | solution.py:300
  101.3 0.8 copy_bitcast_fusion
Async XLA Ops:
  3.3 19.4 %all-to-all-start = ((bf16[8,256,256]{2,1,0:T(8,128)(2,1)}), bf16[8,256,256]{2,1,0:T(8,128)(2,1)S(1)}, u32[]{:S(2)}, u32[]{:S(2)}) async-start(bf16[8,256,256]{2,1,0:T(8,128)(2,1)} %copies.1), calls=%async_computation | async-start | bytes 2097152 | tf_op jit(solution)/shard_map/all_to_all | solution.py:223
  12.6 0.9 copy-start
  13.5 0.7 copy-start.1
  14.1 0.7 copy-start.3
  14.8 0.7 copy-start.4
  15.5 0.7 copy-start.5
  16.2 0.7 copy-start.6
  16.8 0.7 copy-start.7
  22.6 28.0 %copy-start.2 = (s32[1,16]{1,0:T(1,128)S(1)}, s32[1,16]{1,0:T(1,128)}, u32[]{:S(2)}) copy-start(s32[1,16]{1,0:T(1,128)} %coverage.5) | copy-start | bytes 196

commit v5 on v4

--- a/solution.py
+++ b/solution.py
@@ -41,6 +41,10 @@
     return jnp.asarray(np.stack([np.cos(angles), np.sin(angles)]), F32)
 
 
+def sky_index():
+    return lax.axis_index("chip") * CORES + lax.axis_index("core")
+
+
 def dot(left, right):
     return jnp.dot(left, right, preferred_element_type=F32)
 
@@ -52,11 +56,17 @@
     return roots[0, turns], roots[1, turns]
 
 
-def copies_kernel(place, coverage, tiles, copies, own, fetched, stored):
-    sky = place[0]
-    fetch = pltpu.make_async_copy(tiles.at[coverage[0, sky] - sky * TILES_DEV], own, fetched)
-    fetch.start()
-    fetch.wait()
+def copies_kernel(coverage, tiles, copies, covered, near, fetched, stored):
+    sky = sky_index()
+    fetches = (
+        pltpu.make_async_copy(coverage, covered, fetched.at[0]),
+        pltpu.make_async_copy(tiles, near, fetched.at[1]),
+    )
+    for fetch in fetches:
+        fetch.start()
+    for fetch in fetches:
+        fetch.wait()
+    own = near.at[covered[0, sky] - sky * TILES_DEV]
     stores = [pltpu.make_async_copy(own, copies.at[chip], stored.at[chip]) for chip in range(CHIPS)]
     for store in stores:
         store.start()
@@ -138,19 +148,23 @@
     sky_re = (sum_re * shift[0] - sum_im * shift[1]).astype(BF)
     sky_im = (sum_re * shift[1] + sum_im * shift[0]).astype(BF)
     cosines, sines = table[0], table[1]
-    part_re = (dot(sky_re, cosines) - dot(sky_im, sines)).astype(BF)
-    part_im = (dot(sky_re, sines) + dot(sky_im, cosines)).astype(BF)
-    model_re = dot(cosines, part_re) - dot(sines, part_im)
-    model_im = -(dot(sines, part_re) + dot(cosines, part_im))
+    real_rows = jnp.concatenate([cosines, -sines], axis=1)
+    imag_rows = jnp.concatenate([sines, cosines], axis=1)
+    real_cols = jnp.concatenate([cosines, -sines], axis=0)
+    imag_cols = jnp.concatenate([sines, cosines], axis=0)
+    sky_both = jnp.concatenate([sky_re, sky_im], axis=1)
+    part = jnp.concatenate([dot(sky_both, real_cols).astype(BF), dot(sky_both, imag_cols).astype(BF)], axis=0)
+    model_re = dot(real_rows, part)
+    model_im = -dot(imag_rows, part)
 
     res_re = (occupied[0] * (observed[0, 0, 0].astype(F32) - model_re)).astype(BF)
     res_im = (occupied[0] * (observed[0, 0, 1].astype(F32) - model_im)).astype(BF)
     residual[0, 0, 0] = res_re
     residual[0, 0, 1] = res_im
-    part_re = (dot(cosines, res_re) - dot(sines, res_im)).astype(BF)
-    part_im = (dot(sines, res_re) + dot(cosines, res_im)).astype(BF)
-    back_re = dot(part_re, cosines) - dot(part_im, sines)
-    back_im = dot(part_re, sines) + dot(part_im, cosines)
+    res_both = jnp.concatenate([res_re, res_im], axis=0)
+    part = jnp.concatenate([dot(real_rows, res_both).astype(BF), dot(imag_rows, res_both).astype(BF)], axis=1)
+    back_re = dot(part, real_cols)
+    back_im = dot(part, imag_cols)
     turned[0, 0] = (back_re * shift[0] - back_im * shift[1]).astype(BF)
     turned[0, 1] = (back_re * shift[1] + back_im * shift[0]).astype(BF)
 
@@ -202,8 +216,7 @@
 def per_device(
     sky_model, beam, tile_anchor, coverage, unit_chan, unit_block, unit_occupied_mask, observed
 ):
-    chip_core = lax.axis_index("chip") * CORES + lax.axis_index("core")
-    place = chip_core.astype(jnp.int32).reshape(1)
+    place = sky_index().astype(jnp.int32).reshape(1)
     pointings = lax.axis_size("uv")
     anchors = tile_anchor.T
     blocks = jnp.swapaxes(unit_block, 1, 2)
@@ -211,15 +224,16 @@
     copies = pl.pallas_call(
         copies_kernel,
         out_shape=shape((CHIPS, PIXELS, PIXELS), BF),
-        in_specs=[SMEM] * 2 + [pl.BlockSpec(memory_space=pl.ANY)],
+        in_specs=[pl.BlockSpec(memory_space=pl.ANY)] * 2,
         out_specs=pl.BlockSpec(memory_space=pl.ANY),
         scratch_shapes=[
-            pltpu.VMEM((PIXELS, PIXELS), BF),
-            pltpu.SemaphoreType.DMA,
+            pltpu.SMEM((1, UNITS), jnp.int32),
+            pltpu.VMEM((TILES_DEV, PIXELS, PIXELS), BF),
+            pltpu.SemaphoreType.DMA((2,)),
             pltpu.SemaphoreType.DMA((CHIPS,)),
         ],
         name="copies",
-    )(place, coverage, sky_model)
+    )(coverage, sky_model)
     tiles = lax.all_to_all(copies, "chip", 0, 0, tiled=True)
 
     firsts, seconds, phases, occupied = pl.pallas_call(

time: 103 us -> 102 us (level)
  no operation moved by 1% of the time
where the time goes in v5:
time: 102 us
  blocking collectives  72.7 us (71%)
  starting transfers between devices  9.29 us (9%)
  Pallas kernels  9.27 us (9%)
  local copies, waits for them, and re-layouts  5.73 us (6%)
  waiting for transfers between devices  3.84 us (4%)
    all_to_all x1, blocking collectives, per_device(): shares = lax.all_to_all(shares, 'uv', 0, 0, tiled=True)  27.6 us
    all_to_all x1, blocking collectives, per_device(): image = lax.all_to_all(repeated, 'uv', 0, 0, tiled=True)  22.2 us
    all_to_all x1, blocking collectives, per_device(): parts = lax.all_to_all(images, 'chip', 0, 0, tiled=True)  18.5 us
    all_to_all x1, starting transfers between devices, per_device(): tiles = lax.all_to_all(copies, 'chip', 0, 0, tiled=True)  9.29 us
    unnamed x16, local copies, waits for them, and re-layouts  4.91 us
    all_to_all x1, waiting for transfers between devices, per_device(): tiles = lax.all_to_all(copies, 'chip', 0, 0, tiled=True)  3.84 us
    all_gather x1, blocking collectives, per_device(): arrived = lax.all_gather(other, 'core', axis=0, tiled=True)  2.18 us
    all_gather x1, blocking collectives, per_device(): both = lax.all_gather(turned, 'core', axis=0, tiled=True)  2.17 us
  transfers between devices with their start and end apart: 1, of which 1 were waited for; matrix products, arithmetic and copies ran while one was open for 0% of the time, Pallas kernels for 1%

profile of v5, /device:TPU:10, one launch (start us, length us, event | category | flops | bytes accessed | tf_op | source)
XLA Modules:
  0.0 101.6 jit_solution(17025891913745116947)
XLA Ops:
  0.6 2.1 %copies.1 = bf16[8,256,256]{2,1,0:T(8,128)(2,1)} custom-call(s32[1,16]{1,0:T(1,128)} %coverage.5, bf16[4,256,256]{2,1,0:T(8,128)(2,1)} %tiles.1), custom_call_target="tpu_custom_call" | custom-call | tf_op jit(solution)/shard_map/copies/pallas_call | solution.py:224
  2.7 9.3 %all-to-all-start = ((bf16[8,256,256]{2,1,0:T(8,128)(2,1)}), bf16[8,256,256]{2,1,0:T(8,128)(2,1)S(1)}, u32[]{:S(2)}, u32[]{:S(2)}) async-start(bf16[8,256,256]{2,1,0:T(8,128)(2,1)} %copies.1), calls=%async_computation | async-start | bytes 2097152 | tf_op jit(solution)/shard_map/all_to_all | solution.py:237
  12.0 0.0 copy-start
  12.0 0.9 copy-done
  12.9 0.0 copy-start.1
  12.9 0.7 copy-done.1
  13.6 0.0 copy-start.3
  13.6 0.7 copy-done.3
  14.3 0.0 copy-start.4
  14.3 0.7 copy-done.4
  15.0 0.0 copy-start.5
  15.0 0.7 copy-done.5
  15.6 0.0 copy-start.6
  15.6 0.7 copy-done.6
  16.3 0.0 copy-start.7
  16.3 0.7 copy-done.7
  16.9 1.3 %prepare.1 = (f32[256,32]{1,0:T(8,128)S(1)}, f32[32,256]{1,0:T(8,128)S(1)}, f32[2,16]{1,0:T(2,128)S(1)}, f32[1]{0:T(128)}) custom-call(s32[1]{0:T(128)} %bitcast.place, s32[1,16]{1,0:T(1,128)S(1)} %copy-done.1, s32[1,16]{1,0:T(1,128)S(1)} %copy-done.6, s32[1,2,16]{2,1,0:T(2,128)S(1)} %bitcast.8, s32[1,16]{1,0:T(1,128)S(1)} %copy-done.7, ...), custom_call_target="tpu_custom_call" | custom-call | tf_op jit(solution)/shard_map/prepare/pallas_call | solution.py:239
  18.3 3.8 %all-to-all-done.tiles = bf16[8,256,256]{2,1,0:T(8,128)(2,1)S(1)} async-done(((bf16[8,256,256]{2,1,0:T(8,128)(2,1)}), bf16[8,256,256]{2,1,0:T(8,128)(2,1)S(1)}, u32[]{:S(2)}, u32[]{:S(2)}) %all-to-all-start) | async-done | bytes 1048608 | tf_op jit(solution)/shard_map/all_to_all | solution.py:237
  22.1 0.0 copy-start.2
  22.1 2.1 %combine.1 = (f32[2,256,256]{2,1,0:T(8,128)S(1)}, bf16[1,2,256,256]{3,2,1,0:T(8,128)(2,1)S(1)}, f32[2,16,256,256]{3,2,1,0:T(8,128)S(1)}, bf16[1,1,2,256,256]{4,3...) custom-call(s32[1]{0:T(128)} %bitcast.place, f32[2,16]{1,0:T(2,128)S(1)} %get-tuple-element.14.phases, ...), custom_call_target="tpu_custom_call" | custom-call | tf_op jit(solution)/shard_map/combine/pallas_call | solution.py:254
  24.3 2.2 %all_gather.6.arrived = bf16[2,2,256,256]{3,2,1,0:T(8,128)(2,1)S(1)} all-gather(bf16[1,2,256,256]{3,2,1,0:T(8,128)(2,1)S(1)} %get-tuple-element.18), channel_id=1, replica_groups=mesh['chip'=8,'core'=2,'uv'=32] {'core'}, dimensions={0}, use_global_device_ids=true | all-gather | bytes 786432 | tf_op jit(solution)/shard_map/all_gather | solution.py:269
  26.4 2.1 %unit.1 = (bf16[1,1,2,256,256]{4,3,2,1,0:T(8,128)(2,1)}, bf16[1,2,256,256]{3,2,1,0:T(8,128)(2,1)S(1)}) custom-call(s32[1]{0:T(128)} %bitcast.place, f32[1]{0:T(128)} %get-tuple-element.13.occupied, f32[2,256,256]{2,1,0:T(8,128)S(1)} %get-tuple-element.17.own, bf16[2,2,256,256]{3,2,1,0:T(8,128)(2,1)S(1)} %all_gather.6.arrived, ...), custom_call_target="tpu_custom_call" | custom-call | tf_op jit(solution)/shard_map/unit/pallas_call | solution.py:271
  28.6 2.2 %all_gather.7.turned = bf16[2,2,256,256]{3,2,1,0:T(8,128)(2,1)S(1)} all-gather(bf16[1,2,256,256]{3,2,1,0:T(8,128)(2,1)S(1)} %get-tuple-element.22), channel_id=1, replica_groups=mesh['chip'=8,'core'=2,'uv'=32] {'core'}, dimensions={0}, use_global_device_ids=true | all-gather | bytes 786432 | tf_op jit(solution)/shard_map/all_gather | solution.py:283
  30.7 0.8 spread.1
  31.5 18.5 %all_to_all.20.parts = bf16[8,256,256]{2,1,0:T(8,128)(2,1)S(1)} all-to-all(bf16[8,256,256]{2,1,0:T(8,128)(2,1)S(1)} %spread.1), channel_id=1, replica_groups=mesh['chip'=8,'core'=2,'uv'=32] {'chip'}, dimensions={0} | all-to-all | bytes 2097152 | tf_op jit(solution)/shard_map/all_to_all | solution.py:293
  50.0 0.0 copy-done.2
  50.0 0.7 gather.1
  50.7 27.6 %all_to_all.21.shares = bf16[32,8,384]{2,1,0:T(8,128)(2,1)S(1)} all-to-all(bf16[32,8,384]{2,1,0:T(8,128)(2,1)S(1)} %gather.1), channel_id=1, replica_groups=mesh['chip'=8,'core'=2,'uv'=32] {'uv'}, dimensions={0} | all-to-all | bytes 393216 | tf_op jit(solution)/shard_map/all_to_all | solution.py:304
  78.4 0.1 total.1
  78.5 22.2 %all_to_all.22 = bf16[32,4,8,256]{3,2,1,0:T(8,128)(2,1)S(1)} all-to-all(bf16[32,4,8,256]{3,2,1,0:T(8,128)(2,1)S(1)} %total.1), channel_id=1, replica_groups=mesh['chip'=8,'core'=2,'uv'=32] {'uv'}, dimensions={0} | all-to-all | bytes 1048576 | tf_op jit(solution)/shard_map/all_to_all | solution.py:314
  100.7 0.8 copy_bitcast_fusion
Async XLA Ops:
  2.7 19.4 %all-to-all-start = ((bf16[8,256,256]{2,1,0:T(8,128)(2,1)}), bf16[8,256,256]{2,1,0:T(8,128)(2,1)S(1)}, u32[]{:S(2)}, u32[]{:S(2)}) async-start(bf16[8,256,256]{2,1,0:T(8,128)(2,1)} %copies.1), calls=%async_computation | async-start | bytes 2097152 | tf_op jit(solution)/shard_map/all_to_all | solution.py:237
  12.0 0.9 copy-start
  12.9 0.7 copy-start.1
  13.6 0.7 copy-start.3
  14.3 0.7 copy-start.4
  15.0 0.7 copy-start.5
  15.6 0.7 copy-start.6
  16.3 0.7 copy-start.7
  22.1 27.9 %copy-start.2 = (s32[1,16]{1,0:T(1,128)S(1)}, s32[1,16]{1,0:T(1,128)}, u32[]{:S(2)}) copy-start(s32[1,16]{1,0:T(1,128)} %coverage.5) | copy-start | bytes 196

commit v6 on v5

--- a/solution.py
+++ b/solution.py
@@ -43,6 +43,14 @@
 
 def sky_index():
     return lax.axis_index("chip") * CORES + lax.axis_index("core")
+
+
+def uv_groups(pointings):
+    groups = []
+    for sky in range(UNITS):
+        line = range(sky * pointings, (sky + 1) * pointings)
+        groups.append(list(reversed(line)) if sky % CORES else list(line))
+    return groups
 
 
 def dot(left, right):
@@ -301,7 +309,9 @@
         compiler_params=LIMIT,
         name="gather",
     )(place, coverage, parts)
-    shares = lax.all_to_all(shares, "uv", 0, 0, tiled=True)
+    shares = lax.all_to_all(
+        shares, ("chip", "core", "uv"), 0, 0, axis_index_groups=uv_groups(pointings), tiled=True
+    )
 
     repeated = pl.pallas_call(
         total_kernel,
@@ -311,7 +321,9 @@
         compiler_params=LIMIT,
         name="total",
     )(shares)
-    image = lax.all_to_all(repeated, "uv", 0, 0, tiled=True)
+    image = lax.all_to_all(
+        repeated, ("chip", "core", "uv"), 0, 0, axis_index_groups=uv_groups(pointings), tiled=True
+    )
     return residual, jnp.swapaxes(image, 0, 1).reshape(TILES_DEV, PIXELS, PIXELS)
 
 

time: 102 us -> 100 us (0.980)
  the two profiles are of different devices: /device:TPU:10 before, /device:TPU:16 now
where the time goes in v6:
time: 100 us; the launch traced here: 99.8 us
  blocking collectives  70.3 us (70%)
  Pallas kernels  9.27 us (9%)
  waiting for transfers between devices  8.55 us (9%)
  local copies, waits for them, and re-layouts  5.73 us (6%)
  starting transfers between devices  5.32 us (5%)
    all_to_all x1, blocking collectives, per_device(): lax.all_to_all(shares, ('chip', 'core', 'uv'), 0, 0, axis_index_groups=uv...  26.3 us
    all_to_all x1, blocking collectives, per_device(): lax.all_to_all(repeated, ('chip', 'core', 'uv'), 0, 0, axis_index_groups=...  20.2 us
    all_to_all x1, blocking collectives, per_device(): parts = lax.all_to_all(images, 'chip', 0, 0, tiled=True)  19.4 us
    all_to_all x1, waiting for transfers between devices, per_device(): tiles = lax.all_to_all(copies, 'chip', 0, 0, tiled=True)  8.55 us
    all_to_all x1, starting transfers between devices, per_device(): tiles = lax.all_to_all(copies, 'chip', 0, 0, tiled=True)  5.32 us
    unnamed x16, local copies, waits for them, and re-layouts  4.9 us
    all_gather x1, blocking collectives, per_device(): arrived = lax.all_gather(other, 'core', axis=0, tiled=True)  2.18 us
    all_gather x1, blocking collectives, per_device(): both = lax.all_gather(turned, 'core', axis=0, tiled=True)  2.17 us
  transfers between devices with their start and end apart: 1, of which 1 were waited for; matrix products, arithmetic and copies ran while one was open for 0% of the time, Pallas kernels for 1%

profile of v6, /device:TPU:16, one launch (start us, length us, event | category | flops | bytes accessed | tf_op | source)
XLA Modules:
  0.0 99.8 jit_solution(6284812285401266928)
XLA Ops:
  0.6 2.1 %copies.1 = bf16[8,256,256]{2,1,0:T(8,128)(2,1)} custom-call(s32[1,16]{1,0:T(1,128)} %coverage.5, bf16[4,256,256]{2,1,0:T(8,128)(2,1)} %tiles.1), custom_call_target="tpu_custom_call" | custom-call | tf_op jit(solution)/shard_map/copies/pallas_call | solution.py:232
  2.7 5.3 %all-to-all-start = ((bf16[8,256,256]{2,1,0:T(8,128)(2,1)}), bf16[8,256,256]{2,1,0:T(8,128)(2,1)S(1)}, u32[]{:S(2)}, u32[]{:S(2)}) async-start(bf16[8,256,256]{2,1,0:T(8,128)(2,1)} %copies.1), calls=%async_computation | async-start | bytes 2097152 | tf_op jit(solution)/shard_map/all_to_all | solution.py:245
  8.1 0.0 copy-start
  8.1 0.9 copy-done
  9.0 0.0 copy-start.1
  9.0 0.7 copy-done.1
  9.6 0.0 copy-start.3
  9.6 0.7 copy-done.3
  10.3 0.0 copy-start.4
  10.3 0.7 copy-done.4
  11.0 0.0 copy-start.5
  11.0 0.7 copy-done.5
  11.7 0.0 copy-start.6
  11.7 0.7 copy-done.6
  12.3 0.0 copy-start.7
  12.3 0.7 copy-done.7
  13.0 1.3 %prepare.1 = (f32[256,32]{1,0:T(8,128)S(1)}, f32[32,256]{1,0:T(8,128)S(1)}, f32[2,16]{1,0:T(2,128)S(1)}, f32[1]{0:T(128)}) custom-call(s32[1]{0:T(128)} %bitcast.place, s32[1,16]{1,0:T(1,128)S(1)} %copy-done.1, s32[1,16]{1,0:T(1,128)S(1)} %copy-done.6, s32[1,2,16]{2,1,0:T(2,128)S(1)} %bitcast.8, s32[1,16]{1,0:T(1,128)S(1)} %copy-done.7, ...), custom_call_target="tpu_custom_call" | custom-call | tf_op jit(solution)/shard_map/prepare/pallas_call | solution.py:247
  14.3 8.6 %all-to-all-done.tiles = bf16[8,256,256]{2,1,0:T(8,128)(2,1)S(1)} async-done(((bf16[8,256,256]{2,1,0:T(8,128)(2,1)}), bf16[8,256,256]{2,1,0:T(8,128)(2,1)S(1)}, u32[]{:S(2)}, u32[]{:S(2)}) %all-to-all-start) | async-done | bytes 1048608 | tf_op jit(solution)/shard_map/all_to_all | solution.py:245
  22.9 0.0 copy-start.2
  22.9 2.1 %combine.1 = (f32[2,256,256]{2,1,0:T(8,128)S(1)}, bf16[1,2,256,256]{3,2,1,0:T(8,128)(2,1)S(1)}, f32[2,16,256,256]{3,2,1,0:T(8,128)S(1)}, bf16[1,1,2,256,256]{4,3...) custom-call(s32[1]{0:T(128)} %bitcast.place, f32[2,16]{1,0:T(2,128)S(1)} %get-tuple-element.14.phases, ...), custom_call_target="tpu_custom_call" | custom-call | tf_op jit(solution)/shard_map/combine/pallas_call | solution.py:262
  25.0 2.2 %all_gather.6.arrived = bf16[2,2,256,256]{3,2,1,0:T(8,128)(2,1)S(1)} all-gather(bf16[1,2,256,256]{3,2,1,0:T(8,128)(2,1)S(1)} %get-tuple-element.18), channel_id=1, replica_groups=mesh['chip'=8,'core'=2,'uv'=32] {'core'}, dimensions={0}, use_global_device_ids=true | all-gather | bytes 786432 | tf_op jit(solution)/shard_map/all_gather | solution.py:277
  27.2 2.1 %unit.1 = (bf16[1,1,2,256,256]{4,3,2,1,0:T(8,128)(2,1)}, bf16[1,2,256,256]{3,2,1,0:T(8,128)(2,1)S(1)}) custom-call(s32[1]{0:T(128)} %bitcast.place, f32[1]{0:T(128)} %get-tuple-element.13.occupied, f32[2,256,256]{2,1,0:T(8,128)S(1)} %get-tuple-element.17.own, bf16[2,2,256,256]{3,2,1,0:T(8,128)(2,1)S(1)} %all_gather.6.arrived, ...), custom_call_target="tpu_custom_call" | custom-call | tf_op jit(solution)/shard_map/unit/pallas_call | solution.py:279
  29.3 2.2 %all_gather.7.turned = bf16[2,2,256,256]{3,2,1,0:T(8,128)(2,1)S(1)} all-gather(bf16[1,2,256,256]{3,2,1,0:T(8,128)(2,1)S(1)} %get-tuple-element.22), channel_id=1, replica_groups=mesh['chip'=8,'core'=2,'uv'=32] {'core'}, dimensions={0}, use_global_device_ids=true | all-gather | bytes 786432 | tf_op jit(solution)/shard_map/all_gather | solution.py:291
  31.5 0.8 spread.1
  32.3 19.4 %all_to_all.20.parts = bf16[8,256,256]{2,1,0:T(8,128)(2,1)S(1)} all-to-all(bf16[8,256,256]{2,1,0:T(8,128)(2,1)S(1)} %spread.1), channel_id=1, replica_groups=mesh['chip'=8,'core'=2,'uv'=32] {'chip'}, dimensions={0} | all-to-all | bytes 2097152 | tf_op jit(solution)/shard_map/all_to_all | solution.py:301
  51.6 0.0 copy-done.2
  51.6 0.7 gather.1
  52.3 26.3 %all_to_all.21.shares = bf16[32,8,384]{2,1,0:T(8,128)(2,1)S(1)} all-to-all(bf16[32,8,384]{2,1,0:T(8,128)(2,1)S(1)} %gather.1), channel_id=1, replica_groups={{0,1,2,3,4,5,6,7,8,9,10,11,12,13,14,15,16,17,18,19,20,21,22,23,24,25,26..., dimensions={0} | all-to-all | bytes 393216 | tf_op jit(solution)/shard_map/all_to_all | solution.py:312
  78.6 0.1 total.1
  78.8 20.2 %all_to_all.22 = bf16[32,4,8,256]{3,2,1,0:T(8,128)(2,1)S(1)} all-to-all(bf16[32,4,8,256]{3,2,1,0:T(8,128)(2,1)S(1)} %total.1), channel_id=1, replica_groups={{0,1,2,3,4,5,6,7,8,9,10,11,12,13,14,15,16,17,18,19,20,21,22,23,24,25,26..., dimensions={0} | all-to-all | bytes 1048576 | tf_op jit(solution)/shard_map/all_to_all | solution.py:324
  99.0 0.8 copy_bitcast_fusion
Async XLA Ops:
  2.7 20.1 %all-to-all-start = ((bf16[8,256,256]{2,1,0:T(8,128)(2,1)}), bf16[8,256,256]{2,1,0:T(8,128)(2,1)S(1)}, u32[]{:S(2)}, u32[]{:S(2)}) async-start(bf16[8,256,256]{2,1,0:T(8,128)(2,1)} %copies.1), calls=%async_computation | async-start | bytes 2097152 | tf_op jit(solution)/shard_map/all_to_all | solution.py:245
  8.1 0.9 copy-start
  9.0 0.7 copy-start.1
  9.6 0.7 copy-start.3
  10.3 0.7 copy-start.4
  11.0 0.7 copy-start.5
  11.7 0.7 copy-start.6
  12.3 0.7 copy-start.7
  22.9 28.8 %copy-start.2 = (s32[1,16]{1,0:T(1,128)S(1)}, s32[1,16]{1,0:T(1,128)}, u32[]{:S(2)}) copy-start(s32[1,16]{1,0:T(1,128)} %coverage.5) | copy-start | bytes 196

commit v7 on v6

--- a/solution.py
+++ b/solution.py
@@ -17,6 +17,8 @@
 UNITS = CHIPS * CORES
 ROWS = 32
 UNROLL = 2
+BACK_ROWS = 16
+BACK_UNROLL = 8
 MARK = 128
 COSINE = UNITS
 SINE = UNITS + 8
@@ -89,9 +91,9 @@
 
 
 def prepare_kernel(
-    place, coverage, chans, blocks, masks, anchors, roots, beam, firsts, seconds, phases, occupied
+    coverage, chans, blocks, masks, anchors, roots, beam, firsts, seconds, phases, occupied
 ):
-    sky = place[0]
+    sky = sky_index()
     core = lax.bitwise_and(sky, 1)
     occupied[0] = masks[0, sky].astype(F32)
     lines = []
@@ -112,10 +114,10 @@
 
 
 def combine_kernel(
-    place, phases, tiles, firsts, seconds, observed, table,
+    phases, tiles, firsts, seconds, observed, table,
     own, other, weights, observed_near, table_near, near,
 ):
-    core = lax.bitwise_and(place[0], 1)
+    core = lax.axis_index("core")
     fetches = (
         pltpu.make_async_copy(observed, observed_near, near.at[0]),
         pltpu.make_async_copy(table, table_near, near.at[1]),
@@ -145,8 +147,8 @@
         fetch.wait()
 
 
-def unit_kernel(place, occupied, own, arrived, observed, table, firsts, seconds, residual, turned, shift):
-    partner = 1 - lax.bitwise_and(place[0], 1)
+def unit_kernel(occupied, own, arrived, observed, table, firsts, seconds, residual, turned, shift):
+    partner = 1 - lax.axis_index("core")
     row_cos, row_sin = firsts[:, COSINE : COSINE + 1], firsts[:, SINE : SINE + 1]
     col_cos, col_sin = seconds[COSINE : COSINE + 1, :], seconds[SINE : SINE + 1, :]
     shift[0] = row_cos * col_cos - row_sin * col_sin
@@ -178,9 +180,9 @@
 
 
 def spread_kernel(turned, weights, images):
-    @pl.loop(0, PIXELS // ROWS, unroll=UNROLL)
+    @pl.loop(0, PIXELS // BACK_ROWS, unroll=BACK_UNROLL)
     def step(at):
-        rows = pl.ds(pl.multiple_of(at * ROWS, ROWS), ROWS)
+        rows = pl.ds(pl.multiple_of(at * BACK_ROWS, BACK_ROWS), BACK_ROWS)
         planes = [[turned[e, plane, rows, :].astype(F32) for plane in range(2)] for e in range(CORES)]
         for chip in range(CHIPS):
             total = None
@@ -191,8 +193,8 @@
             images[chip, rows, :] = total.astype(BF)
 
 
-def gather_kernel(place, coverage, parts, shares):
-    sky = place[0]
+def gather_kernel(coverage, parts, shares):
+    sky = sky_index()
     position = (coverage[0, sky] - sky * TILES_DEV).astype(F32)
     pointings, share = shares.shape[0], shares.shape[1]
     total = parts[0].astype(F32)
@@ -224,7 +226,6 @@
 def per_device(
     sky_model, beam, tile_anchor, coverage, unit_chan, unit_block, unit_occupied_mask, observed
 ):
-    place = sky_index().astype(jnp.int32).reshape(1)
     pointings = lax.axis_size("uv")
     anchors = tile_anchor.T
     blocks = jnp.swapaxes(unit_block, 1, 2)
@@ -252,11 +253,11 @@
             shape((2, UNITS), F32),
             shape((1,), F32),
         ),
-        in_specs=[SMEM] * 7 + [VMEM],
+        in_specs=[SMEM] * 6 + [VMEM],
         out_specs=(VMEM, VMEM, SMEM, SMEM),
         compiler_params=LIMIT,
         name="prepare",
-    )(place, coverage, unit_chan, blocks, unit_occupied_mask, anchors, anchor_roots(), beam)
+    )(coverage, unit_chan, blocks, unit_occupied_mask, anchors, anchor_roots(), beam)
 
     far = pltpu.with_memory_space_constraint
     own, other, weights, observed_near, table_near = pl.pallas_call(
@@ -268,12 +269,12 @@
             shape((1, 1, 2, PIXELS, PIXELS), BF),
             shape((2, PIXELS, PIXELS), BF),
         ),
-        in_specs=[SMEM] * 2 + [VMEM] * 3 + [pl.BlockSpec(memory_space=pltpu.HBM)] * 2,
+        in_specs=[SMEM] + [VMEM] * 3 + [pl.BlockSpec(memory_space=pltpu.HBM)] * 2,
         out_specs=(VMEM,) * 5,
         scratch_shapes=[pltpu.SemaphoreType.DMA((2,))],
         compiler_params=LIMIT,
         name="combine",
-    )(place, phases, tiles, firsts, seconds, far(observed, pltpu.HBM), far(dft_matrix(), pltpu.HBM))
+    )(phases, tiles, firsts, seconds, far(observed, pltpu.HBM), far(dft_matrix(), pltpu.HBM))
     arrived = lax.all_gather(other, "core", axis=0, tiled=True)
 
     residual, turned = pl.pallas_call(
@@ -282,12 +283,12 @@
             shape((1, 1, 2, PIXELS, PIXELS), BF),
             shape((1, 2, PIXELS, PIXELS), BF),
         ),
-        in_specs=[SMEM] * 2 + [VMEM] * 6,
+        in_specs=[SMEM] + [VMEM] * 6,
         out_specs=(VMEM, VMEM),
         scratch_shapes=[pltpu.VMEM((2, PIXELS, PIXELS), F32)],
         compiler_params=LIMIT,
         name="unit",
-    )(place, occupied, own, arrived, observed_near, table_near, firsts, seconds)
+    )(occupied, own, arrived, observed_near, table_near, firsts, seconds)
     both = lax.all_gather(turned, "core", axis=0, tiled=True)
 
     images = pl.pallas_call(
@@ -304,11 +305,11 @@
     shares = pl.pallas_call(
         gather_kernel,
         out_shape=shape((pointings, share, PIXELS + MARK), BF),
-        in_specs=[SMEM] * 2 + [VMEM],
+        in_specs=[SMEM, VMEM],
         out_specs=VMEM,
         compiler_params=LIMIT,
         name="gather",
-    )(place, coverage, parts)
+    )(coverage, parts)
     shares = lax.all_to_all(
         shares, ("chip", "core", "uv"), 0, 0, axis_index_groups=uv_groups(pointings), tiled=True
     )

time: 100 us -> 100 us (level)
  no operation moved by 1% of the time
where the time goes in v7:
time: 100 us; the launch traced here: 99.7 us
  blocking collectives  70.3 us (70%)
  Pallas kernels  9.12 us (9%)
  waiting for transfers between devices  8.54 us (9%)
  local copies, waits for them, and re-layouts  5.73 us (6%)
  starting transfers between devices  5.32 us (5%)
    all_to_all x1, blocking collectives, per_device(): lax.all_to_all(shares, ('chip', 'core', 'uv'), 0, 0, axis_index_groups=uv...  26.3 us
    all_to_all x1, blocking collectives, per_device(): lax.all_to_all(repeated, ('chip', 'core', 'uv'), 0, 0, axis_index_groups=...  20.2 us
    all_to_all x1, blocking collectives, per_device(): parts = lax.all_to_all(images, 'chip', 0, 0, tiled=True)  19.4 us
    all_to_all x1, waiting for transfers between devices, per_device(): tiles = lax.all_to_all(copies, 'chip', 0, 0, tiled=True)  8.54 us
    all_to_all x1, starting transfers between devices, per_device(): tiles = lax.all_to_all(copies, 'chip', 0, 0, tiled=True)  5.32 us
    unnamed x16, local copies, waits for them, and re-layouts  4.9 us
    all_gather x1, blocking collectives, per_device(): arrived = lax.all_gather(other, 'core', axis=0, tiled=True)  2.18 us
    all_gather x1, blocking collectives, per_device(): both = lax.all_gather(turned, 'core', axis=0, tiled=True)  2.17 us
  transfers between devices with their start and end apart: 1, of which 1 were waited for; matrix products, arithmetic and copies ran while one was open for 0% of the time, Pallas kernels for 1%

profile of v7, /device:TPU:16, one launch (start us, length us, event | category | flops | bytes accessed | tf_op | source)
XLA Modules:
  0.0 99.7 jit_solution(4078487212375158570)
XLA Ops:
  0.6 2.1 %copies.1 = bf16[8,256,256]{2,1,0:T(8,128)(2,1)} custom-call(s32[1,16]{1,0:T(1,128)} %coverage.5, bf16[4,256,256]{2,1,0:T(8,128)(2,1)} %tiles.1), custom_call_target="tpu_custom_call" | custom-call | tf_op jit(solution)/shard_map/copies/pallas_call | solution.py:233
  2.7 5.3 %all-to-all-start = ((bf16[8,256,256]{2,1,0:T(8,128)(2,1)}), bf16[8,256,256]{2,1,0:T(8,128)(2,1)S(1)}, u32[]{:S(2)}, u32[]{:S(2)}) async-start(bf16[8,256,256]{2,1,0:T(8,128)(2,1)} %copies.1), calls=%async_computation | async-start | bytes 2097152 | tf_op jit(solution)/shard_map/all_to_all | solution.py:246
  8.1 0.0 copy-start
  8.1 0.9 copy-done
  9.0 0.0 copy-start.1
  9.0 0.7 copy-done.1
  9.6 0.0 copy-start.3
  9.6 0.7 copy-done.3
  10.3 0.0 copy-start.4
  10.3 0.7 copy-done.4
  11.0 0.0 copy-start.5
  11.0 0.7 copy-done.5
  11.7 0.0 copy-start.6
  11.7 0.7 copy-done.6
  12.3 0.0 copy-start.7
  12.3 0.7 copy-done.7
  13.0 1.3 %prepare.1 = (f32[256,32]{1,0:T(8,128)S(1)}, f32[32,256]{1,0:T(8,128)S(1)}, f32[2,16]{1,0:T(2,128)S(1)}, f32[1]{0:T(128)}) custom-call(s32[1,16]{1,0:T(1,128)S(1)} %copy-done.1, s32[1,16]{1,0:T(1,128)S(1)} %copy-done.6, s32[1,2,16]{2,1,0:T(2,128)S(1)} %bitcast.7, s32[1,16]{1,0:T(1,128)S(1)} %copy-done.7, s32[2,64]{1,0:T(2,128)S(1)} %bitcast.8, ...), custom_call_target="tpu_custom_call" | custom-call | tf_op jit(solution)/shard_map/prepare/pallas_call | solution.py:248
  14.3 8.5 %all-to-all-done.tiles = bf16[8,256,256]{2,1,0:T(8,128)(2,1)S(1)} async-done(((bf16[8,256,256]{2,1,0:T(8,128)(2,1)}), bf16[8,256,256]{2,1,0:T(8,128)(2,1)S(1)}, u32[]{:S(2)}, u32[]{:S(2)}) %all-to-all-start) | async-done | bytes 1048608 | tf_op jit(solution)/shard_map/all_to_all | solution.py:246
  22.9 0.0 copy-start.2
  22.9 2.1 %combine.1 = (f32[2,256,256]{2,1,0:T(8,128)S(1)}, bf16[1,2,256,256]{3,2,1,0:T(8,128)(2,1)S(1)}, f32[2,16,256,256]{3,2,1,0:T(8,128)S(1)}, bf16[1,1,2,256,256]{4,3...) custom-call(f32[2,16]{1,0:T(2,128)S(1)} %get-tuple-element.14.phases, bf16[8,256,256]{2,1,0:T(8,128)(2,1)S(1)} %all-to-all-done.tiles, ...), custom_call_target="tpu_custom_call" | custom-call | tf_op jit(solution)/shard_map/combine/pallas_call | solution.py:263
  25.0 2.2 %all_gather.6.arrived = bf16[2,2,256,256]{3,2,1,0:T(8,128)(2,1)S(1)} all-gather(bf16[1,2,256,256]{3,2,1,0:T(8,128)(2,1)S(1)} %get-tuple-element.18), channel_id=1, replica_groups=mesh['chip'=8,'core'=2,'uv'=32] {'core'}, dimensions={0}, use_global_device_ids=true | all-gather | bytes 786432 | tf_op jit(solution)/shard_map/all_gather | solution.py:278
  27.2 2.1 %unit.1 = (bf16[1,1,2,256,256]{4,3,2,1,0:T(8,128)(2,1)}, bf16[1,2,256,256]{3,2,1,0:T(8,128)(2,1)S(1)}) custom-call(f32[1]{0:T(128)} %get-tuple-element.13.occupied, f32[2,256,256]{2,1,0:T(8,128)S(1)} %get-tuple-element.17.own, bf16[2,2,256,256]{3,2,1,0:T(8,128)(2,1)S(1)} %all_gather.6.arrived, bf16[1,1,2,256,256]{4,3,2,1,0:T(8,128)(2,1)S(1)} %get-tuple-element.19.observed, ...), custom_call_target="tpu_custom_call" | custom-call | tf_op jit(solution)/shard_map/unit/pallas_call | solution.py:280
  29.3 2.2 %all_gather.7.turned = bf16[2,2,256,256]{3,2,1,0:T(8,128)(2,1)S(1)} all-gather(bf16[1,2,256,256]{3,2,1,0:T(8,128)(2,1)S(1)} %get-tuple-element.22), channel_id=1, replica_groups=mesh['chip'=8,'core'=2,'uv'=32] {'core'}, dimensions={0}, use_global_device_ids=true | all-gather | bytes 786432 | tf_op jit(solution)/shard_map/all_gather | solution.py:292
  31.5 0.6 spread.1
  32.1 19.4 %all_to_all.20.parts = bf16[8,256,256]{2,1,0:T(8,128)(2,1)S(1)} all-to-all(bf16[8,256,256]{2,1,0:T(8,128)(2,1)S(1)} %spread.1), channel_id=1, replica_groups=mesh['chip'=8,'core'=2,'uv'=32] {'chip'}, dimensions={0} | all-to-all | bytes 2097152 | tf_op jit(solution)/shard_map/all_to_all | solution.py:302
  51.5 0.0 copy-done.2
  51.5 0.7 gather.1
  52.2 26.3 %all_to_all.21.shares = bf16[32,8,384]{2,1,0:T(8,128)(2,1)S(1)} all-to-all(bf16[32,8,384]{2,1,0:T(8,128)(2,1)S(1)} %gather.1), channel_id=1, replica_groups={{0,1,2,3,4,5,6,7,8,9,10,11,12,13,14,15,16,17,18,19,20,21,22,23,24,25,26..., dimensions={0} | all-to-all | bytes 393216 | tf_op jit(solution)/shard_map/all_to_all | solution.py:313
  78.5 0.1 total.1
  78.6 20.2 %all_to_all.22 = bf16[32,4,8,256]{3,2,1,0:T(8,128)(2,1)S(1)} all-to-all(bf16[32,4,8,256]{3,2,1,0:T(8,128)(2,1)S(1)} %total.1), channel_id=1, replica_groups={{0,1,2,3,4,5,6,7,8,9,10,11,12,13,14,15,16,17,18,19,20,21,22,23,24,25,26..., dimensions={0} | all-to-all | bytes 1048576 | tf_op jit(solution)/shard_map/all_to_all | solution.py:325
  98.8 0.8 copy_bitcast_fusion
Async XLA Ops:
  2.7 20.1 %all-to-all-start = ((bf16[8,256,256]{2,1,0:T(8,128)(2,1)}), bf16[8,256,256]{2,1,0:T(8,128)(2,1)S(1)}, u32[]{:S(2)}, u32[]{:S(2)}) async-start(bf16[8,256,256]{2,1,0:T(8,128)(2,1)} %copies.1), calls=%async_computation | async-start | bytes 2097152 | tf_op jit(solution)/shard_map/all_to_all | solution.py:246
  8.1 0.9 copy-start
  9.0 0.7 copy-start.1
  9.6 0.7 copy-start.3
  10.3 0.7 copy-start.4
  11.0 0.7 copy-start.5
  11.7 0.7 copy-start.6
  12.3 0.7 copy-start.7
  22.9 28.6 %copy-start.2 = (s32[1,16]{1,0:T(1,128)S(1)}, s32[1,16]{1,0:T(1,128)}, u32[]{:S(2)}) copy-start(s32[1,16]{1,0:T(1,128)} %coverage.5) | copy-start | bytes 196

commit v8 on v7

--- a/solution.py
+++ b/solution.py
@@ -91,11 +91,13 @@
 
 
 def prepare_kernel(
-    coverage, chans, blocks, masks, anchors, roots, beam, firsts, seconds, phases, occupied
+    coverage, chans, blocks, masks, anchors, roots, beam, firsts, seconds, phases, facts
 ):
     sky = sky_index()
     core = lax.bitwise_and(sky, 1)
-    occupied[0] = masks[0, sky].astype(F32)
+    position = coverage[0, sky] - sky * TILES_DEV
+    facts[0:8, :] = jnp.full((8, PIXELS), masks[0, sky].astype(F32))
+    facts[8:16, :] = jnp.full((8, PIXELS), position.astype(F32))
     lines = []
     for e in range(CORES):
         unit = sky - core + e
@@ -147,7 +149,7 @@
         fetch.wait()
 
 
-def unit_kernel(occupied, own, arrived, observed, table, firsts, seconds, residual, turned, shift):
+def unit_kernel(facts, own, arrived, observed, table, firsts, seconds, residual, turned, shift):
     partner = 1 - lax.axis_index("core")
     row_cos, row_sin = firsts[:, COSINE : COSINE + 1], firsts[:, SINE : SINE + 1]
     col_cos, col_sin = seconds[COSINE : COSINE + 1, :], seconds[SINE : SINE + 1, :]
@@ -167,8 +169,9 @@
     model_re = dot(real_rows, part)
     model_im = -dot(imag_rows, part)
 
-    res_re = (occupied[0] * (observed[0, 0, 0].astype(F32) - model_re)).astype(BF)
-    res_im = (occupied[0] * (observed[0, 0, 1].astype(F32) - model_im)).astype(BF)
+    occupied = facts[0:1, :]
+    res_re = (occupied * (observed[0, 0, 0].astype(F32) - model_re)).astype(BF)
+    res_im = (occupied * (observed[0, 0, 1].astype(F32) - model_im)).astype(BF)
     residual[0, 0, 0] = res_re
     residual[0, 0, 1] = res_im
     res_both = jnp.concatenate([res_re, res_im], axis=0)
@@ -193,15 +196,14 @@
             images[chip, rows, :] = total.astype(BF)
 
 
-def gather_kernel(coverage, parts, shares):
-    sky = sky_index()
-    position = (coverage[0, sky] - sky * TILES_DEV).astype(F32)
+def gather_kernel(facts, parts, shares):
     pointings, share = shares.shape[0], shares.shape[1]
     total = parts[0].astype(F32)
     for chip in range(1, CHIPS):
         total += parts[chip].astype(F32)
     shares[:, :, 0:PIXELS] = total.reshape(pointings, share, PIXELS).astype(BF)
-    shares[:, :, PIXELS:] = jnp.full((pointings, share, MARK), position, F32).astype(BF)
+    mark = facts[8:9, 0:MARK].reshape(1, 1, MARK)
+    shares[:, :, PIXELS:] = jnp.broadcast_to(mark, (pointings, share, MARK)).astype(BF)
 
 
 def total_kernel(shares, repeated):
@@ -245,16 +247,16 @@
     )(coverage, sky_model)
     tiles = lax.all_to_all(copies, "chip", 0, 0, tiled=True)
 
-    firsts, seconds, phases, occupied = pl.pallas_call(
+    firsts, seconds, phases, facts = pl.pallas_call(
         prepare_kernel,
         out_shape=(
             shape((PIXELS, LINES), F32),
             shape((LINES, PIXELS), F32),
             shape((2, UNITS), F32),
-            shape((1,), F32),
+            shape((16, PIXELS), F32),
         ),
         in_specs=[SMEM] * 6 + [VMEM],
-        out_specs=(VMEM, VMEM, SMEM, SMEM),
+        out_specs=(VMEM, VMEM, SMEM, VMEM),
         compiler_params=LIMIT,
         name="prepare",
     )(coverage, unit_chan, blocks, unit_occupied_mask, anchors, anchor_roots(), beam)
@@ -283,12 +285,12 @@
             shape((1, 1, 2, PIXELS, PIXELS), BF),
             shape((1, 2, PIXELS, PIXELS), BF),
         ),
-        in_specs=[SMEM] + [VMEM] * 6,
+        in_specs=[VMEM] * 7,
         out_specs=(VMEM, VMEM),
         scratch_shapes=[pltpu.VMEM((2, PIXELS, PIXELS), F32)],
         compiler_params=LIMIT,
         name="unit",
-    )(occupied, own, arrived, observed_near, table_near, firsts, seconds)
+    )(facts, own, arrived, observed_near, table_near, firsts, seconds)
     both = lax.all_gather(turned, "core", axis=0, tiled=True)
 
     images = pl.pallas_call(
@@ -305,11 +307,11 @@
     shares = pl.pallas_call(
         gather_kernel,
         out_shape=shape((pointings, share, PIXELS + MARK), BF),
-        in_specs=[SMEM, VMEM],
+        in_specs=[VMEM] * 2,
         out_specs=VMEM,
         compiler_params=LIMIT,
         name="gather",
-    )(coverage, parts)
+    )(facts, parts)
     shares = lax.all_to_all(
         shares, ("chip", "core", "uv"), 0, 0, axis_index_groups=uv_groups(pointings), tiled=True
     )

time: 100 us -> 98.8 us (0.988)
  Pallas kernels: 9.12 us -> 7.91 us
    unnamed x16 -> x14, local copies, waits for them, and re-layouts: 4.9 us -> 4.9 us
where the time goes in v8:
time: 98.8 us; the launch traced here: 98.4 us
  blocking collectives  70.3 us (71%)
  waiting for transfers between devices  8.54 us (9%)
  Pallas kernels  7.91 us (8%)
  local copies, waits for them, and re-layouts  5.73 us (6%)
  starting transfers between devices  5.32 us (5%)
    all_to_all x1, blocking collectives, per_device(): lax.all_to_all(shares, ('chip', 'core', 'uv'), 0, 0, axis_index_groups=uv...  26.3 us
    all_to_all x1, blocking collectives, per_device(): lax.all_to_all(repeated, ('chip', 'core', 'uv'), 0, 0, axis_index_groups=...  20.2 us
    all_to_all x1, blocking collectives, per_device(): parts = lax.all_to_all(images, 'chip', 0, 0, tiled=True)  19.4 us
    all_to_all x1, waiting for transfers between devices, per_device(): tiles = lax.all_to_all(copies, 'chip', 0, 0, tiled=True)  8.54 us
    all_to_all x1, starting transfers between devices, per_device(): tiles = lax.all_to_all(copies, 'chip', 0, 0, tiled=True)  5.32 us
    unnamed x14, local copies, waits for them, and re-layouts  4.9 us
    all_gather x1, blocking collectives, per_device(): arrived = lax.all_gather(other, 'core', axis=0, tiled=True)  2.18 us
    all_gather x1, blocking collectives, per_device(): both = lax.all_gather(turned, 'core', axis=0, tiled=True)  2.17 us
  transfers between devices with their start and end apart: 1, of which 1 were waited for; matrix products, arithmetic and copies ran while one was open for 0% of the time, Pallas kernels for 1%

profile of v8, /device:TPU:16, one launch (start us, length us, event | category | flops | bytes accessed | tf_op | source)
XLA Modules:
  0.0 98.4 jit_solution(17800623475117824698)
XLA Ops:
  0.6 2.1 %copies.1 = bf16[8,256,256]{2,1,0:T(8,128)(2,1)} custom-call(s32[1,16]{1,0:T(1,128)} %coverage.3, bf16[4,256,256]{2,1,0:T(8,128)(2,1)} %tiles.1), custom_call_target="tpu_custom_call" | custom-call | tf_op jit(solution)/shard_map/copies/pallas_call | solution.py:235
  2.7 5.3 %all-to-all-start = ((bf16[8,256,256]{2,1,0:T(8,128)(2,1)}), bf16[8,256,256]{2,1,0:T(8,128)(2,1)S(1)}, u32[]{:S(2)}, u32[]{:S(2)}) async-start(bf16[8,256,256]{2,1,0:T(8,128)(2,1)} %copies.1), calls=%async_computation | async-start | bytes 2097152 | tf_op jit(solution)/shard_map/all_to_all | solution.py:248
  8.1 0.0 copy-start
  8.1 0.9 copy-done
  9.0 0.0 copy-start.1
  9.0 0.7 copy-done.1
  9.6 0.0 copy-start.2
  9.6 0.7 copy-done.2
  10.3 0.0 copy-start.3
  10.3 0.7 copy-done.3
  11.0 0.0 copy-start.4
  11.0 0.7 copy-done.4
  11.7 0.0 copy-start.5
  11.7 0.7 copy-done.5
  12.3 0.0 copy-start.6
  12.3 0.7 copy-done.6
  13.0 1.3 %prepare.1 = (f32[256,32]{1,0:T(8,128)S(1)}, f32[32,256]{1,0:T(8,128)S(1)}, f32[2,16]{1,0:T(2,128)S(1)}, f32[16,256]{1,0:T(8,128)S(1)}) custom-call(s32[1,16]{1,0:T(1,128)S(1)} %copy-done.1, s32[1,16]{1,0:T(1,128)S(1)} %copy-done.5, s32[1,2,16]{2,1,0:T(2,128)S(1)} %bitcast.7, s32[1,16]{1,0:T(1,128)S(1)} %copy-done.6, s32[2,64]{1,0:T(2,128)S(1)} %bitcast.8, ...), custom_call_target="tpu_custom_call" | custom-call | tf_op jit(solution)/shard_map/prepare/pallas_call | solution.py:250
  14.3 8.5 %all-to-all-done.tiles = bf16[8,256,256]{2,1,0:T(8,128)(2,1)S(1)} async-done(((bf16[8,256,256]{2,1,0:T(8,128)(2,1)}), bf16[8,256,256]{2,1,0:T(8,128)(2,1)S(1)}, u32[]{:S(2)}, u32[]{:S(2)}) %all-to-all-start) | async-done | bytes 1048608 | tf_op jit(solution)/shard_map/all_to_all | solution.py:248
  22.9 2.1 %combine.1 = (f32[2,256,256]{2,1,0:T(8,128)S(1)}, bf16[1,2,256,256]{3,2,1,0:T(8,128)(2,1)S(1)}, f32[2,16,256,256]{3,2,1,0:T(8,128)S(1)}, bf16[1,1,2,256,256]{4,3...) custom-call(f32[2,16]{1,0:T(2,128)S(1)} %get-tuple-element.14.phases, bf16[8,256,256]{2,1,0:T(8,128)(2,1)S(1)} %all-to-all-done.tiles, ...), custom_call_target="tpu_custom_call" | custom-call | tf_op jit(solution)/shard_map/combine/pallas_call | solution.py:265
  25.0 2.2 %all_gather.6.arrived = bf16[2,2,256,256]{3,2,1,0:T(8,128)(2,1)S(1)} all-gather(bf16[1,2,256,256]{3,2,1,0:T(8,128)(2,1)S(1)} %get-tuple-element.18), channel_id=1, replica_groups=mesh['chip'=8,'core'=2,'uv'=32] {'core'}, dimensions={0}, use_global_device_ids=true | all-gather | bytes 786432 | tf_op jit(solution)/shard_map/all_gather | solution.py:280
  27.2 1.4 %unit.1 = (bf16[1,1,2,256,256]{4,3,2,1,0:T(8,128)(2,1)}, bf16[1,2,256,256]{3,2,1,0:T(8,128)(2,1)S(1)}) custom-call(f32[16,256]{1,0:T(8,128)S(1)} %get-tuple-element.13.facts, f32[2,256,256]{2,1,0:T(8,128)S(1)} %get-tuple-element.17.own, bf16[2,2,256,256]{3,2,1,0:T(8,128)(2,1)S(1)} %all_gather.6.arrived, ...), custom_call_target="tpu_custom_call" | custom-call | tf_op jit(solution)/shard_map/unit/pallas_call | solution.py:282
  28.6 2.2 %all_gather.7.turned = bf16[2,2,256,256]{3,2,1,0:T(8,128)(2,1)S(1)} all-gather(bf16[1,2,256,256]{3,2,1,0:T(8,128)(2,1)S(1)} %get-tuple-element.22), channel_id=1, replica_groups=mesh['chip'=8,'core'=2,'uv'=32] {'core'}, dimensions={0}, use_global_device_ids=true | all-gather | bytes 786432 | tf_op jit(solution)/shard_map/all_gather | solution.py:294
  30.8 0.6 spread.1
  31.4 19.4 %all_to_all.20.parts = bf16[8,256,256]{2,1,0:T(8,128)(2,1)S(1)} all-to-all(bf16[8,256,256]{2,1,0:T(8,128)(2,1)S(1)} %spread.1), channel_id=1, replica_groups=mesh['chip'=8,'core'=2,'uv'=32] {'chip'}, dimensions={0} | all-to-all | bytes 2097152 | tf_op jit(solution)/shard_map/all_to_all | solution.py:304
  50.8 0.1 gather.1
  50.9 26.3 %all_to_all.21.shares = bf16[32,8,384]{2,1,0:T(8,128)(2,1)S(1)} all-to-all(bf16[32,8,384]{2,1,0:T(8,128)(2,1)S(1)} %gather.1), channel_id=1, replica_groups={{0,1,2,3,4,5,6,7,8,9,10,11,12,13,14,15,16,17,18,19,20,21,22,23,24,25,26..., dimensions={0} | all-to-all | bytes 393216 | tf_op jit(solution)/shard_map/all_to_all | solution.py:315
  77.3 0.1 total.1
  77.4 20.2 %all_to_all.22 = bf16[32,4,8,256]{3,2,1,0:T(8,128)(2,1)S(1)} all-to-all(bf16[32,4,8,256]{3,2,1,0:T(8,128)(2,1)S(1)} %total.1), channel_id=1, replica_groups={{0,1,2,3,4,5,6,7,8,9,10,11,12,13,14,15,16,17,18,19,20,21,22,23,24,25,26..., dimensions={0} | all-to-all | bytes 1048576 | tf_op jit(solution)/shard_map/all_to_all | solution.py:327
  97.6 0.8 copy_bitcast_fusion
Async XLA Ops:
  2.7 20.1 %all-to-all-start = ((bf16[8,256,256]{2,1,0:T(8,128)(2,1)}), bf16[8,256,256]{2,1,0:T(8,128)(2,1)S(1)}, u32[]{:S(2)}, u32[]{:S(2)}) async-start(bf16[8,256,256]{2,1,0:T(8,128)(2,1)} %copies.1), calls=%async_computation | async-start | bytes 2097152 | tf_op jit(solution)/shard_map/all_to_all | solution.py:248
  8.1 0.9 copy-start
  9.0 0.7 copy-start.1
  9.6 0.7 copy-start.2
  10.3 0.7 copy-start.3
  11.0 0.7 copy-start.4
  11.7 0.7 copy-start.5
  12.3 0.7 copy-start.6
